TPU v7x, 256 devices: a whole 4x4x8 slice. The times are simulated.
256 devices in a mesh: wide: 32 (over y, x, core), narrow: 8 (over z).
Axes of the slice: x: 4, y: 4, z: 8, core: 2. Of those that a mesh axis runs over, the one named last changes fastest.
Arguments:
- noise: float32 [1024, 1024, 128], P('narrow', 'wide'), may hold values from -6 to 6
- spectrum: float32 [128, 1024, 1024], P('wide', None, 'narrow'), may hold values from 0.1 to 8.5, as said below
- assay: bfloat16 [256, 512], P(('wide', 'narrow')), may hold values from -5 to 5
- measure_weights: bfloat16 [256, 512, 4, 128], P(('wide', 'narrow')), may hold values from -3 to 3
- measure_owner: int32 [256, 512], P(('wide', 'narrow')), may hold values from 0 to 255, as said below
- measure_cell: int32 [256, 512], P(('wide', 'narrow')), may hold values from 0 to 524287
- measure_pencils: int32 [256, 512, 4], P(('wide', 'narrow')), may hold values from 0 to 4095
Outputs:
- conditioned: float32 [1024, 1024, 128], P('narrow', 'wide')
Inputs may be any that keep to these rules, and one draw needn't show every extreme that they name: `spectrum`: Positive, with rough factors from frequency to frequency. `measure_owner`: devices are numbered with narrow fastest. At most 8 measurements of one device share an owner; one owner, drawn from the seed, receives exactly 8 from every device. `measure_cell`: cells of the owner's block are numbered with z fastest, then y, then x. `measure_pencils`: pencils of the owner's block are numbered with y fastest.
All inputs are finite; a program needn't handle non-finite values.
Results may differ from a plain program's by a relative error of at most 0.0003.
Values may be sent and summed in bfloat16 or wider, within the bound.
A program may use at most 128 MiB of HBM per device.

v0:
```python
import math

import jax
import jax.numpy as jnp
from jax import lax
from jax.sharding import PartitionSpec as P

CELLS_FIRST = 1024
CELLS_SECOND = 1024
CELLS_THIRD = 128
TARGET_PENCILS = 4


highest = lax.Precision.HIGHEST


def pair_tables(cosine, sine):
    upper = jnp.stack([cosine, sine], axis=1)
    lower = jnp.stack([-sine, cosine], axis=1)
    return jnp.stack([upper, lower])


def dft_matrix(length, sign):
    index = jnp.arange(length, dtype=jnp.int32)
    phase = index[:, None] * index[None, :] % length
    angle = phase.astype(jnp.float32) * (2.0 * math.pi / length)
    return pair_tables(jnp.cos(angle), sign * jnp.sin(angle))


def slot_depth(depth, half):
    slots = jnp.arange(depth, dtype=jnp.int32)
    span = 2 * half
    base = slots // span * half + slots % span % half
    mirror = jnp.where(base > 0, depth - base, depth // 2)
    return jnp.where(slots % span < half, base, mirror)


def arranged_tables(depth, half, sign):
    depth_of = slot_depth(depth, half)
    cell_list = jnp.arange(depth, dtype=jnp.int32)
    phase = depth_of[:, None] * cell_list[None, :] % depth
    angle = phase.astype(jnp.float32) * (2.0 * math.pi / depth)
    return (jnp.cos(angle), sign * jnp.sin(angle))


def transform(block, sign):
    outer = block.shape[1]
    length = block.shape[2]
    inner = block.shape[3]
    rows_q = 128
    rows_p = length // rows_q
    four = block.reshape(2, outer, rows_p, rows_q, inner)
    four = jnp.einsum("sapqb,sptc->tacqb", four, dft_matrix(rows_p, sign), precision=highest)
    index_p = jnp.arange(rows_p, dtype=jnp.int32)
    index_q = jnp.arange(rows_q, dtype=jnp.int32)
    angle = (index_p[:, None] * index_q[None, :] % length).astype(jnp.float32) * (
        2.0 * math.pi / length
    )
    twist_cos = jnp.cos(angle)[None, :, :, None]
    twist_sin = (sign * jnp.sin(angle))[None, :, :, None]
    four = jnp.stack(
        [four[0] * twist_cos - four[1] * twist_sin, four[0] * twist_sin + four[1] * twist_cos]
    )
    four = jnp.einsum("sacqb,sqtd->tadcb", four, dft_matrix(rows_q, sign), precision=highest)
    return four.reshape(2, outer, length, inner)


def rows_then_turn(block):
    return jnp.swapaxes(transform(block, -1.0), 2, 3)


def forward_along(block):
    return transform(block, -1.0)


def turn_then_rows(block):
    return transform(jnp.swapaxes(block, 2, 3), 1.0)


def local(noise, spectrum, assay, measure_weights, measure_owner, measure_cell, measure_pencils):
    size_x, size_y, depth = noise.shape
    half = spectrum.shape[0] // 2
    tables = jnp.stack(arranged_tables(depth, half, -1.0))
    spectral = jnp.einsum("xyz,sqz->sqyx", noise, tables, precision=highest)
    spectral = rows_then_turn(
        lax.all_to_all(spectral, "wide", split_axis=1, concat_axis=2, tiled=True)
    )
    spectral = forward_along(
        lax.all_to_all(spectral, "narrow", split_axis=3, concat_axis=2, tiled=True)
    )
    scaled = spectrum * (1.0 / (CELLS_FIRST * CELLS_SECOND * CELLS_THIRD))
    spectral = transform(spectral * scaled[None], 1.0)
    spectral = turn_then_rows(
        lax.all_to_all(spectral, "narrow", split_axis=2, concat_axis=3, tiled=True)
    )
    cos_rows, sin_rows = arranged_tables(depth, half, 1.0)
    inverse_tables = jnp.stack([cos_rows, -sin_rows])
    field = jnp.einsum(
        "sqyx,sqz->xyz",
        lax.all_to_all(spectral, "wide", split_axis=2, concat_axis=1, tiled=True),
        inverse_tables,
        precision=highest,
    )
    n_wide = lax.axis_size("wide")
    n_narrow = lax.axis_size("narrow")
    owner_device = measure_owner.reshape(-1)
    count = owner_device.shape[0]
    capacity = max(4, 4 * count // (n_wide * n_narrow))
    row_index = jnp.arange(count, dtype=jnp.int32)
    earlier = row_index[None, :] < row_index[:, None]
    same_owner = owner_device[None, :] == owner_device[:, None]
    slot_position = jnp.sum(same_owner & earlier, axis=1, dtype=jnp.int32)
    wide_target = owner_device // n_narrow
    narrow_target = owner_device % n_narrow
    weight_holder = jnp.zeros((n_wide, n_narrow, capacity, TARGET_PENCILS, depth), jnp.bfloat16)
    weight_holder = weight_holder.at[wide_target, narrow_target, slot_position].set(
        measure_weights[0]
    )
    assay_buf = jnp.zeros((n_wide, n_narrow, capacity), jnp.bfloat16)
    assay_buf = assay_buf.at[wide_target, narrow_target, slot_position].set(assay[0])
    row_indices = jnp.concatenate([measure_cell[0][:, None], measure_pencils[0]], axis=1)
    index_buf = jnp.zeros((n_wide, n_narrow, capacity, TARGET_PENCILS + 1), jnp.int32)
    index_buf = index_buf.at[wide_target, narrow_target, slot_position].set(row_indices)
    weight_got, assay_got, index_got = (
        lax.all_to_all(
            lax.all_to_all(weight_holder, "wide", split_axis=0, concat_axis=0, tiled=True),
            "narrow",
            split_axis=1,
            concat_axis=1,
            tiled=True,
        ),
        lax.all_to_all(
            lax.all_to_all(assay_buf, "wide", split_axis=0, concat_axis=0, tiled=True),
            "narrow",
            split_axis=1,
            concat_axis=1,
            tiled=True,
        ),
        lax.all_to_all(
            lax.all_to_all(index_buf, "wide", split_axis=0, concat_axis=0, tiled=True),
            "narrow",
            split_axis=1,
            concat_axis=1,
            tiled=True,
        ),
    )
    index_got = index_got.reshape(-1, TARGET_PENCILS + 1)
    cell_list = index_got[:, 0]
    targets = index_got[:, 1:].reshape(-1)
    value = field.reshape(-1)[cell_list]
    resid = assay_got.reshape(-1).astype(jnp.float32) - value
    contrib = resid[:, None, None] * weight_got.reshape(-1, TARGET_PENCILS, depth).astype(
        jnp.float32
    )
    correction = (
        jnp.zeros((size_x * size_y, depth), jnp.float32).at[targets].add(contrib.reshape(-1, depth))
    )
    return field + correction.reshape(size_x, size_y, depth)


def solution(mesh):
    placed = (
        P("narrow", "wide", None),
        P("wide", None, "narrow"),
        P(("wide", "narrow"), None),
        P(("wide", "narrow"), None, None, None),
        P(("wide", "narrow"), None),
        P(("wide", "narrow"), None),
        P(("wide", "narrow"), None, None),
    )
    return jax.shard_map(
        local, mesh=mesh, in_specs=placed, out_specs=P("narrow", "wide", None), check_vma=False
    )
```

profile of v0, /device:TPU:65, one launch (start us, length us, event | category | flops | bytes accessed | tf_op | source)
XLA Modules:
  0.0 598.4 jit_solution(5593420963950159069)
XLA Ops:
  1.6 6.0 %convolution_bitcast_fusion = f32[2,128,32,128]{3,1,2,0:T(8,128)S(1)} fusion(f32[128,32,128]{2,1,0:T(8,128)} %param.7, f32[1,128,128]{2,1,0:T(8,128)S(1)} %get-tuple-element.23, f32[1,128,128]{2,1,0:T(8,128)S(1)} %get-tuple-element.22), kind=kOutput, calls=%fused_computation.45 | convolution fusion | flops 1610645504 | bytes 6422528 | tf_op jit(solution)/shard_map/xyz,sqz->sqyx/dot_general | solution.py:84
  12.1 8.6 %all-to-all-start = ((f32[2,128,32,128]{3,2,0,1:T(8,128)}), f32[2,128,32,128]{3,2,0,1:T(8,128)}, u32[]{:S(2)}, u32[]{:S(2)}) async-start(f32[2,128,32,128]{3,2,0,1:T(8,128)} %copy.272), calls=%async_computation | async-start | bytes 8388608 | tf_op jit(solution)/shard_map/all_to_all | solution.py:86
  22.0 28.0 %scatter_fusion = s32[32,8,8,5]{3,2,1,0:T(8,128)S(1)} fusion(s32[32,8,8,5]{3,2,1,0:T(8,128)S(1)} %broadcast_in_dim.15, s32[512]{0:T(512)S(1)} %bitcast.210, s32[512,5]{1,0:T(8,128)S(1)} %copy.300), kind=kCustom, calls=%fused_computation.1 | custom fusion | bytes 36864 | tf_op jit(solution)/shard_map/scatter | solution.py:123
  52.8 29.6 %scatter_fusion.1 = bf16[32,8,8]{0,2,1:T(8,128)(2,1)S(1)} fusion(bf16[32,8,8]{0,2,1:T(8,128)(2,1)S(1)} %broadcast_in_dim.16, s32[512]{0:T(512)S(1)} %bitcast.211, bf16[512]{0:T(512)(128)(2,1)S(1)} %reduce), kind=kCustom, calls=%fused_computation.2 | custom fusion | bytes 9216 | tf_op jit(solution)/shard_map/scatter | solution.py:120
  84.0 7.4 %all-to-all-start.6 = ((bf16[32,8,8]{2,1,0:T(8,128)(2,1)}), bf16[32,8,8]{2,1,0:T(8,128)(2,1)S(1)}, u32[]{:S(2)}, u32[]{:S(2)}) async-start(bf16[32,8,8]{2,1,0:T(8,128)(2,1)} %copy.305), calls=%async_computation.6 | async-start | bytes 131072 | tf_op jit(solution)/shard_map/all_to_all | solution.py:133
  94.2 5.6 fusion.24
  102.6 7.6 %all-to-all-start.4 = ((s32[32,1,320]{2,1,0:T(1,128)}), s32[32,1,320]{2,1,0:T(1,128)S(1)}, u32[]{:S(2)}, u32[]{:S(2)}) async-start(s32[32,1,320]{2,1,0:T(1,128)} %reshape.696), calls=%async_computation.4 | async-start | bytes 98304 | tf_op jit(solution)/shard_map/all_to_all | solution.py:140
  110.2 6.6 %fusion.27 = f32[2,4,128,8,128]{4,2,3,1,0:T(8,128)S(1)} fusion(f32[2,4,8,128,128]{4,2,3,1,0:T(8,128)} %pad_maximum_fusion, f32[1,128,2,128]{1,3,0,2:T(8,128)S(1)} %get-tuple-element.14, f32[1,128,2,128]{1,3,0,2:T(8,128)S(1)} %get-tuple-element.15), kind=kOutput, calls=%fused_computation.38 | convolution fusion | flops 3221291008 | bytes 8650752 | tf_op jit(solution)/shard_map/sacqb,sqtd->tadcb/dot_general | solution.py:64
  123.8 7.7 %all-to-all-start.1 = ((f32[2,4,128,1024]{2,1,0,3:T(4,128)}), f32[2,4,128,1024]{2,1,0,3:T(4,128)}, u32[]{:S(2)}, u32[]{:S(2)}) async-start(f32[2,4,128,1024]{2,1,0,3:T(4,128)} %copy.280), calls=%async_computation.1 | async-start | bytes 8388608 | tf_op jit(solution)/shard_map/all_to_all | solution.py:89
  134.7 58.1 %scatter_fusion.2 = bf16[32,8,8,4,128]{4,3,2,1,0:T(4,128)(2,1)} fusion(bf16[32,8,8,4,128]{4,3,2,1,0:T(4,128)(2,1)} %broadcast_in_dim.17, s32[512]{0:T(512)S(1)} %bitcast.212, bf16[512,4,128]{2,1,0:T(4,128)(2,1)S(1)} %bitcast.229), kind=kCustom, calls=%fused_computation.3 | custom fusion | bytes 1579008 | tf_op jit(solution)/shard_map/scatter | solution.py:116
  197.9 27.3 %all-to-all-done.1 = f32[2,4,128,1024]{2,1,0,3:T(4,128)} async-done(((f32[2,4,128,1024]{2,1,0,3:T(4,128)}), f32[2,4,128,1024]{2,1,0,3:T(4,128)}, u32[]{:S(2)}, u32[]{:S(2)}) %all-to-all-start.1) | async-done | bytes 4194336 | tf_op jit(solution)/shard_map/all_to_all | solution.py:89
  225.3 6.3 %all-to-all-start.7 = ((bf16[8,2,128]{2,1,0:T(2,128)(2,1)}), bf16[8,2,128]{2,1,0:T(2,128)(2,1)S(1)}, u32[]{:S(2)}, u32[]{:S(2)}) async-start(bf16[8,2,128]{2,1,0:T(2,128)(2,1)} %reshape.694), calls=%async_computation.7 | async-start | bytes 8192 | tf_op jit(solution)/shard_map/all_to_all | solution.py:132
  235.8 7.8 %fusion.45 = f32[2,4,8,128,128]{4,2,3,1,0:T(8,128)} fusion(f32[2,4,128,8,128]{4,3,0,2,1:T(8,128)} %copy.336, f32[1,8,2,8]{1,3,0,2:T(8,128)S(1)} %copy.270, f32[1,8,2,8]{1,3,0,2:T(8,128)S(1)} %copy.269), kind=kOutput, calls=%fused_computation.44 | convolution fusion | flops 201326848 | bytes 8389632 | tf_op jit(solution)/shard_map/sapqb,sptc->tacqb/dot_general | solution.py:53
  243.7 6.7 %all-to-all-start.5 = ((s32[8,1,1280]{2,1,0:T(1,128)}), s32[8,1,1280]{2,1,0:T(1,128)S(1)}, u32[]{:S(2)}, u32[]{:S(2)}) async-start(s32[8,1,1280]{2,1,0:T(1,128)} %reshape.698), calls=%async_computation.5 | async-start | bytes 81920 | tf_op jit(solution)/shard_map/all_to_all | solution.py:139
  255.1 9.6 %all-to-all-start.8 = ((bf16[32,8,8,4,128]{4,3,2,1,0:T(4,128)(2,1)}), bf16[32,8,8,4,128]{4,3,2,1,0:T(4,128)(2,1)}, u32[]{:S(2)}, u32[]{:S(2)}) async-start(bf16[32,8,8,4,128]{4,3,2,1,0:T(4,128)(2,1)} %scatter_fusion.2), calls=%async_computation.8 | async-start | bytes 4194304 | tf_op jit(solution)/shard_map/all_to_all | solution.py:126
  274.7 5.8 fusion.33
  292.6 7.1 %all-to-all-start.2 = ((f32[2,4,1024,128]{3,1,0,2:T(4,128)}), f32[2,4,1024,128]{3,1,0,2:T(4,128)}, u32[]{:S(2)}, u32[]{:S(2)}) async-start(f32[2,4,1024,128]{3,1,0,2:T(4,128)} %copy.289), calls=%async_computation.2 | async-start | bytes 8388608 | tf_op jit(solution)/shard_map/all_to_all | solution.py:94
  303.5 89.4 %all-to-all-done.2 = f32[2,4,1024,128]{3,1,0,2:T(4,128)} async-done(((f32[2,4,1024,128]{3,1,0,2:T(4,128)}), f32[2,4,1024,128]{3,1,0,2:T(4,128)}, u32[]{:S(2)}, u32[]{:S(2)}) %all-to-all-start.2) | async-done | bytes 4194336 | tf_op jit(solution)/shard_map/all_to_all | solution.py:94
  392.9 7.0 %all-to-all-start.9 = ((bf16[32,8,8,4,128]{4,3,2,0,1:T(4,128)(2,1)}), bf16[32,8,8,4,128]{4,3,2,0,1:T(4,128)(2,1)S(1)}, u32[]{:S(2)}, u32[]{:S(2)}) async-start(bf16[32,8,8,4,128]{4,3,2,0,1:T(4,128)(2,1)} %copy.309), calls=%async_computation.9 | async-start | bytes 4194304 | tf_op jit(solution)/shard_map/all_to_all | solution.py:125
  427.9 20.9 %all-to-all-done.9 = bf16[32,8,8,4,128]{4,3,2,0,1:T(4,128)(2,1)S(1)} async-done(((bf16[32,8,8,4,128]{4,3,2,0,1:T(4,128)(2,1)}), bf16[32,8,8,4,128]{4,3,2,0,1:T(4,128)(2,1)S(1)}, u32[]{:S(2)}, u32[]{:S(2)}) %all-to-all-start.9) | async-done | bytes 2097184 | tf_op jit(solution)/shard_map/all_to_all | solution.py:125
  448.8 6.5 %all-to-all-start.3 = ((f32[2,4,1024,128]{3,1,0,2:T(4,128)}), f32[2,4,1024,128]{3,1,0,2:T(4,128)}, u32[]{:S(2)}, u32[]{:S(2)}) async-start(f32[2,4,1024,128]{3,1,0,2:T(4,128)} %copy.296), calls=%async_computation.3 | async-start | bytes 8388608 | tf_op jit(solution)/shard_map/all_to_all | solution.py:100
  462.3 43.1 %all-to-all-done.3 = f32[2,4,1024,128]{3,1,0,2:T(4,128)} async-done(((f32[2,4,1024,128]{3,1,0,2:T(4,128)}), f32[2,4,1024,128]{3,1,0,2:T(4,128)}, u32[]{:S(2)}, u32[]{:S(2)}) %all-to-all-start.3) | async-done | bytes 4194336 | tf_op jit(solution)/shard_map/all_to_all | solution.py:100
  517.1 11.8 %gather_fusion = f32[2048]{0:T(1024)S(1)} fusion(f32[524288]{0:T(1024)S(1)} %bitcast.213, s32[2048]{0:T(1024)S(1)} %broadcast_clamp_fusion), kind=kCustom, calls=%fused_computation | custom fusion | bytes 24576 | tf_op jit(solution)/shard_map/gather | solution.py:150
  529.9 59.1 %scatter_custom_fusion.3 = f32[4096,128]{1,0:T(8,128)} fusion(s32[8192]{0:T(1024)S(1)} %bitcast.232, f32[8192,128]{1,0:T(8,128)} %bitcast.214, f32[8192]{0:T(1024)S(1)} %mul.834, f32[]{:T(128)} %constant.178.clone.1), kind=kCustom, calls=%fused_computation.35 | custom fusion | flops 2097152 | bytes 6324228 | tf_op jit(solution)/shard_map/scatter-add | solution.py:156
  (120 shorter events, 123.8 us)
Async XLA Ops:
  1.0 0.6 copy-start.1
  12.1 9.3 %copy-start.9 = (s32[1,512,4]{1,2,0:T(4,128)S(1)}, s32[1,512,4]{1,2,0:T(4,128)}, u32[]{:S(2)}) copy-start(s32[1,512,4]{1,2,0:T(4,128)} %param.13) | copy-start | bytes 24580
  12.1 9.3 %copy-start.11 = (s32[1,512]{1,0:T(1,128)S(1)}, s32[1,512]{1,0:T(1,128)}, u32[]{:S(2)}) copy-start(s32[1,512]{1,0:T(1,128)} %param.12) | copy-start | bytes 6148
  12.1 9.5 %copy-start.8 = (s32[1,512]{1,0:T(1,128)S(1)}, s32[1,512]{1,0:T(1,128)}, u32[]{:S(2)}) copy-start(s32[1,512]{1,0:T(1,128)} %param.11) | copy-start | bytes 6148
  12.1 71.9 %all-to-all-start = ((f32[2,128,32,128]{3,2,0,1:T(8,128)}), f32[2,128,32,128]{3,2,0,1:T(8,128)}, u32[]{:S(2)}, u32[]{:S(2)}) async-start(f32[2,128,32,128]{3,2,0,1:T(8,128)} %copy.272), calls=%async_computation | async-start | bytes 8388608 | tf_op jit(solution)/shard_map/all_to_all | solution.py:86
  21.4 78.4 %copy-start.3 = (f32[8,128]{0,1:T(8,128)}, f32[8,128]{0,1:T(8,128)S(1)}, u32[]{:S(2)}) copy-start(f32[8,128]{0,1:T(8,128)S(1)} %copy.277) | copy-start | bytes 12292
  21.4 31.3 %copy-start.10 = (bf16[1,512]{1,0:T(2,128)(2,1)S(1)}, bf16[1,512]{1,0:T(2,128)(2,1)}, u32[]{:S(2)}) copy-start(bf16[1,512]{1,0:T(2,128)(2,1)} %param.9) | copy-start | bytes 3076
  84.0 18.6 %all-to-all-start.6 = ((bf16[32,8,8]{2,1,0:T(8,128)(2,1)}), bf16[32,8,8]{2,1,0:T(8,128)(2,1)S(1)}, u32[]{:S(2)}, u32[]{:S(2)}) async-start(bf16[32,8,8]{2,1,0:T(8,128)(2,1)} %copy.305), calls=%async_computation.6 | async-start | bytes 131072 | tf_op jit(solution)/shard_map/all_to_all | solution.py:133
  102.6 21.2 %all-to-all-start.4 = ((s32[32,1,320]{2,1,0:T(1,128)}), s32[32,1,320]{2,1,0:T(1,128)S(1)}, u32[]{:S(2)}, u32[]{:S(2)}) async-start(s32[32,1,320]{2,1,0:T(1,128)} %reshape.696), calls=%async_computation.4 | async-start | bytes 98304 | tf_op jit(solution)/shard_map/all_to_all | solution.py:140
  123.8 10.9 %copy-start.6 = (bf16[1,512,4,128]{3,2,1,0:T(4,128)(2,1)S(1)}, bf16[1,512,4,128]{3,2,1,0:T(4,128)(2,1)}, u32[]{:S(2)}) copy-start(bf16[1,512,4,128]{3,2,1,0:T(4,128)(2,1)} %param.10) | copy-start | bytes 1572868
  123.8 101.5 %all-to-all-start.1 = ((f32[2,4,128,1024]{2,1,0,3:T(4,128)}), f32[2,4,128,1024]{2,1,0,3:T(4,128)}, u32[]{:S(2)}, u32[]{:S(2)}) async-start(f32[2,4,128,1024]{2,1,0,3:T(4,128)} %copy.280), calls=%async_computation.1 | async-start | bytes 8388608 | tf_op jit(solution)/shard_map/all_to_all | solution.py:89
  225.3 18.4 %all-to-all-start.7 = ((bf16[8,2,128]{2,1,0:T(2,128)(2,1)}), bf16[8,2,128]{2,1,0:T(2,128)(2,1)S(1)}, u32[]{:S(2)}, u32[]{:S(2)}) async-start(bf16[8,2,128]{2,1,0:T(2,128)(2,1)} %reshape.694), calls=%async_computation.7 | async-start | bytes 8192 | tf_op jit(solution)/shard_map/all_to_all | solution.py:132
  235.8 14.5 %copy-start.4 = (f32[8,128]{0,1:T(8,128)S(1)}, f32[8,128]{0,1:T(8,128)}, u32[]{:S(2)}) copy-start(f32[8,128]{0,1:T(8,128)} %copy-done.3) | copy-start | bytes 12292
  243.7 11.5 %all-to-all-start.5 = ((s32[8,1,1280]{2,1,0:T(1,128)}), s32[8,1,1280]{2,1,0:T(1,128)S(1)}, u32[]{:S(2)}, u32[]{:S(2)}) async-start(s32[8,1,1280]{2,1,0:T(1,128)} %reshape.698), calls=%async_computation.5 | async-start | bytes 81920 | tf_op jit(solution)/shard_map/all_to_all | solution.py:139
  255.1 37.4 %all-to-all-start.8 = ((bf16[32,8,8,4,128]{4,3,2,1,0:T(4,128)(2,1)}), bf16[32,8,8,4,128]{4,3,2,1,0:T(4,128)(2,1)}, u32[]{:S(2)}, u32[]{:S(2)}) async-start(bf16[32,8,8,4,128]{4,3,2,1,0:T(4,128)(2,1)} %scatter_fusion.2), calls=%async_computation.8 | async-start | bytes 4194304 | tf_op jit(solution)/shard_map/all_to_all | solution.py:126
  274.7 5.8 copy-start.5
  292.6 100.4 %all-to-all-start.2 = ((f32[2,4,1024,128]{3,1,0,2:T(4,128)}), f32[2,4,1024,128]{3,1,0,2:T(4,128)}, u32[]{:S(2)}, u32[]{:S(2)}) async-start(f32[2,4,1024,128]{3,1,0,2:T(4,128)} %copy.289), calls=%async_computation.2 | async-start | bytes 8388608 | tf_op jit(solution)/shard_map/all_to_all | solution.py:94
  392.9 55.9 %all-to-all-start.9 = ((bf16[32,8,8,4,128]{4,3,2,0,1:T(4,128)(2,1)}), bf16[32,8,8,4,128]{4,3,2,0,1:T(4,128)(2,1)S(1)}, u32[]{:S(2)}, u32[]{:S(2)}) async-start(bf16[32,8,8,4,128]{4,3,2,0,1:T(4,128)(2,1)} %copy.309), calls=%async_computation.9 | async-start | bytes 4194304 | tf_op jit(solution)/shard_map/all_to_all | solution.py:125
  448.8 56.6 %all-to-all-start.3 = ((f32[2,4,1024,128]{3,1,0,2:T(4,128)}), f32[2,4,1024,128]{3,1,0,2:T(4,128)}, u32[]{:S(2)}, u32[]{:S(2)}) async-start(f32[2,4,1024,128]{3,1,0,2:T(4,128)} %copy.296), calls=%async_computation.3 | async-start | bytes 8388608 | tf_op jit(solution)/shard_map/all_to_all | solution.py:100
  508.4 2.7 copy-start.2
  508.4 2.7 copy-start.7
  529.9 62.1 %copy-start = (f32[128,32,128]{0,2,1:T(8,128)S(1)}, f32[128,32,128]{0,2,1:T(8,128)}, u32[]{:S(2)}) copy-start(f32[128,32,128]{0,2,1:T(8,128)} %convolution_bitcast_fusion.1) | copy-start | bytes 6291460
where the time goes:
time: 610 us; the launch traced here: 598 us
  local copies, waits for them, and re-layouts  208 us (34%)
  waiting for transfers between devices  181 us (30%)
  other arithmetic  81.2 us (13%)
  starting transfers between devices  74.6 us (12%)
  matrix products  53.3 us (9%)
    all_to_all x1, waiting for transfers between devices, local(): lax.all_to_all(spectral, 'narrow', split_axis=2, concat_axis=3, tiled=True)  89.4 us
    scatter-add x1, other arithmetic, local(): jnp.zeros((size_x * size_y, depth), jnp.float32).at[targets]  59.1 us
    scatter x1, local copies, waits for them, and re-layouts, local(): weight_holder.at[wide_target, narrow_target, slot_position]  58.1 us
    all_to_all x1, waiting for transfers between devices, local(): lax.all_to_all(spectral, 'wide', split_axis=2, concat_axis=1, tiled=True)  43.1 us
    scatter x2, local copies, waits for them, and re-layouts, local(): assay_buf.at[wide_target, narrow_target, slot_position].set(assay[0])  30.3 us
    scatter x2, local copies, waits for them, and re-layouts, local(): index_buf.at[wide_target, narrow_target, slot_position].set(row_indices)  29.7 us
    all_to_all x1, waiting for transfers between devices, local(): lax.all_to_all(spectral, 'narrow', split_axis=3, concat_axis=2, tiled=True)  27.3 us
    dot_general x4, matrix products, transform(): jnp.einsum('sapqb,sptc->tacqb', four, dft_matrix(rows_p, sign), precision...  24.6 us
  transfers between devices with their start and end apart: 10, of which 4 were waited for; matrix products, arithmetic and copies ran while one was open for 40% of the time, Pallas kernels for 0%

commit v1 on v0

v1 whole, which is shorter than its diff:
```python
import math

import jax
import jax.numpy as jnp
import ml_dtypes
import numpy as np
from jax import lax
from jax.experimental import pallas as pl
from jax.experimental.pallas import tpu as pltpu
from jax.sharding import PartitionSpec as P

NX, NY, NZ = 1024, 1024, 128
TARGETS = 4
WIDE, NARROW = 32, 8
SLOTS = 2
MESH = pl.DeviceIdType.MESH
f32, bf16, i32 = jnp.float32, jnp.bfloat16, jnp.int32

LN2 = math.log(2.0)
CODE = 16.0 / LN2
PEAK = 32600.0
TINY = 1e-30
SPEC_LOW = math.log(0.1)
SPEC_CODE = 65000.0 / math.log(85.0)
ROOT_HALF = math.sqrt(0.5)


def split(a):
    high = a.astype(ml_dtypes.bfloat16)
    low = (a - high.astype(np.float64)).astype(ml_dtypes.bfloat16)
    return high, low


def pair_matrix(sign):
    index = np.arange(128)
    angle = 2 * np.pi * (index[:, None] * index[None, :] % 128) / 128
    c, s = np.cos(angle), sign * np.sin(angle)
    return np.block([[c, -s], [s, c]])


def depth_forward():
    kz = 2 * np.arange(32)[None, :] + np.arange(2)[:, None]
    kz = kz.reshape(-1)
    z = np.arange(128)
    angle = 2 * np.pi * (kz[:, None] * z[None, :] % 128) / 128
    re, im = np.cos(angle), -np.sin(angle)
    im[kz == 0] = np.cos(np.pi * z)
    return np.concatenate([re, im], 0)


def depth_inverse():
    kz = (2 * np.arange(32)[None, :] + np.arange(2)[:, None]).reshape(-1)
    z = np.arange(128)
    angle = 2 * np.pi * (kz[:, None] * z[None, :] % 128) / 128
    re, im = 2 * np.cos(angle), -2 * np.sin(angle)
    re[kz == 0] = 1.0
    im[kz == 0] = np.cos(np.pi * z)
    return np.concatenate([re, im], 0)


def make_tables():
    h, l = split(depth_forward())
    tz = np.concatenate([h, l, h], 1)
    h, l = split(depth_inverse())
    tzi = np.concatenate([h, l, h], 0)
    yf = np.stack(split(pair_matrix(-1.0)))
    yi = np.stack(split(pair_matrix(1.0)))
    xf = np.stack(split(pair_matrix(-1.0).T))
    xi = np.stack(split(pair_matrix(1.0).T))
    c = np.arange(8)
    a = np.arange(128)
    angle = 2 * np.pi * c[:, None] * a[None, :] / 1024
    tx = np.stack([np.cos(angle), np.sin(angle)]).astype(np.float32)
    row = np.arange(128)
    lane_of = 8 * (row % 16) + row // 16
    own = np.zeros((128, 128))
    own[row, lane_of] = 1
    mir = np.zeros((128, 128))
    mir[row, (128 - lane_of) % 128] = 1
    own2 = np.concatenate([own, own], 1).astype(ml_dtypes.bfloat16)
    flips = np.zeros((2, 128, 128))
    flips[0, (128 - row) % 128, row] = 1
    flips[1, 127 - row, row] = 1
    flips = np.concatenate([flips, flips], 1).astype(ml_dtypes.bfloat16)
    return dict(
        tz=tz, tzi=tzi, yf=yf, yi=yi, xf=xf, xi=xi, tx=tx, own2=own2,
        mir=mir.astype(ml_dtypes.bfloat16), flips=flips,
    )


TABLES = make_tables()


def halves(v):
    h = v.astype(bf16)
    return h, (v - h.astype(f32)).astype(bf16)


def times_i(v, sign):
    re, im = v
    return (-im, re) if sign > 0 else (im, -re)


def add(a, b):
    return a[0] + b[0], a[1] + b[1]


def sub(a, b):
    return a[0] - b[0], a[1] - b[1]


def dft4(v, sign):
    s, d = add(v[0], v[2]), sub(v[0], v[2])
    t, u = add(v[1], v[3]), times_i(sub(v[1], v[3]), sign)
    return [add(s, t), add(d, u), sub(s, t), sub(d, u)]


def dft8(v, sign):
    e = dft4(v[0::2], sign)
    o = dft4(v[1::2], sign)
    g = float(sign)
    re, im = o[1]
    o[1] = ((re - g * im) * ROOT_HALF, (im + g * re) * ROOT_HALF)
    o[2] = times_i(o[2], sign)
    re, im = o[3]
    o[3] = ((-re - g * im) * ROOT_HALF, (g * re - im) * ROOT_HALF)
    return [add(e[c], o[c]) for c in range(4)] + [sub(e[c], o[c]) for c in range(4)]


def turn(v, cos, sin, sign):
    re, im = v
    if sign < 0:
        return re * cos + im * sin, im * cos - re * sin
    return re * cos - im * sin, im * cos + re * sin


def scale_code(m):
    return jnp.ceil(jnp.log(jnp.maximum(m, TINY)) * CODE).astype(i32)


def encode_factor(code):
    return jnp.exp(code.astype(f32) * (-1.0 / CODE)) * PEAK


def decode_factor(code):
    return jnp.exp(code.astype(f32) * (1.0 / CODE)) * (1.0 / PEAK)


def pack(re, im):
    a = jnp.round(re).astype(i32)
    b = jnp.round(im).astype(i32)
    return (a << 16) | (b & 0xFFFF)


def unpack(word):
    return (word >> 16).astype(f32), ((word << 16) >> 16).astype(f32)


def tile_max(tiles):
    tiles = [jnp.abs(t) for t in tiles]
    while len(tiles) > 1:
        tiles = [jnp.maximum(a, b) for a, b in zip(tiles[0::2], tiles[1::2])] + (
            tiles[-1:] if len(tiles) % 2 else []
        )
    return tiles[0]


def mm(a, b):
    return jnp.dot(a, b, preferred_element_type=f32)


def mm_t(a, b):
    return lax.dot_general(a, b, (((1,), (1,)), ((), ())), preferred_element_type=f32)


def rows(start, size):
    return pl.ds(pl.multiple_of(start, 8), size)


def rows16(start, size):
    return pl.ds(pl.multiple_of(start, 16), size)


def spectral_kernel(
    noise, spec, tz, yf, yi, xf, xi, tyc, tys, tx, own2, mir, flips,
    out,
    zre, zim, ws, wr, bh, bl, big, big2, ns, nr, lh, ll, ms, mr, us,
    ear, bsp, vs, vr, vc,
    w_send, w_recv, n_send, n_recv, m_send, m_recv, u_send, u_recv, v_send, v_recv,
):
    me_w = lax.axis_index("wide")
    me_n = lax.axis_index("narrow")
    special = me_w == 0
    edge = special & ((me_n == 0) | (me_n == 4))

    barrier = pltpu.get_barrier_semaphore()

    def greet_wide(i, _):
        pl.semaphore_signal(
            barrier, inc=1, device_id={"wide": lax.rem(me_w + i, WIDE)}, device_id_type=MESH
        )
        return 0

    def greet_narrow(i, _):
        pl.semaphore_signal(
            barrier, inc=1, device_id={"narrow": lax.rem(me_n + i, NARROW)}, device_id_type=MESH
        )
        return 0

    lax.fori_loop(1, WIDE, greet_wide, 0)
    lax.fori_loop(1, NARROW, greet_narrow, 0)

    def wide_copy(src, dst, sends, recvs, s, peer, slot):
        return pltpu.make_async_remote_copy(
            src_ref=src.at[s, peer], dst_ref=dst.at[s, slot], send_sem=sends.at[s, peer],
            recv_sem=recvs.at[s, slot], device_id={"wide": peer}, device_id_type=MESH,
        )

    def narrow_copy(src, dst, sends, recvs, s, peer, slot):
        return pltpu.make_async_remote_copy(
            src_ref=src.at[s, peer], dst_ref=dst.at[s, slot], send_sem=sends.at[s, peer],
            recv_sem=recvs.at[s, slot], device_id={"narrow": peer}, device_id_type=MESH,
        )

    def send_all(make, count, me, args, s):
        def one(i, _):
            make(*args, s, lax.rem(me + i, count), me).start()
            return 0

        lax.fori_loop(1, count, one, 0)

    def recv_all(make, count, me, args, s):
        def one(i, _):
            peer = lax.rem(me + i, count)
            make(*args, s, peer, peer).wait_recv()
            return 0

        lax.fori_loop(1, count, one, 0)

    def sent_all(make, count, me, args, s):
        def one(i, _):
            peer = lax.rem(me + i, count)
            make(*args, s, peer, peer).wait_send()
            return 0

        lax.fori_loop(1, count, one, 0)

    w_args = (ws, wr, w_send, w_recv)
    n_args = (ns, nr, n_send, n_recv)
    m_args = (ms, mr, m_send, m_recv)
    u_args = (us, out, u_send, u_recv)

    def depth(y, _):
        h, l = halves(noise[pl.ds(y, 128, stride=32), :])
        res = mm_t(tz[...], jnp.concatenate([h, h, l], axis=1))
        zre[pl.ds(y, 64, stride=32), :] = res[:64]
        zim[pl.ds(y, 64, stride=32), :] = res[64:]
        return 0

    lax.fori_loop(0, 32, depth, 0)

    def code_wide(read, dst, s, w, to):
        re, im = read(w)
        m = tile_max([re[8 * t : 8 * t + 8] for t in range(4)] + [im[8 * t : 8 * t + 8] for t in range(4)])
        code = scale_code(m)
        fac = encode_factor(code)
        for t in range(4):
            sl = slice(8 * t, 8 * t + 8)
            dst[s, to, 8 * t : 8 * t + 8, :] = pack(re[sl] * fac, im[sl] * fac)
        dst[s, to, 32:40, :] = code

    for s in range(SLOTS):
        def read_depth(w, s=s):
            at = rows((s * 32 + w) * 32, 32)
            return zre[at, :], zim[at, :]

        def code_one(w, _, s=s, read=read_depth):
            code_wide(read, ws, s, w, w)
            return 0

        lax.fori_loop(0, WIDE, code_one, 0)
        wr[s, me_w] = ws[s, me_w]
        if s == 0:
            pl.semaphore_wait(barrier, WIDE - 1 + NARROW - 1)
        send_all(wide_copy, WIDE, me_w, w_args, s)

    late = special & (me_n >= 4)
    own_slots = (jnp.where(late, 2, 0), 1)
    mir_slots = (jnp.where(special & (me_n < 4), 2, jnp.where(special, 0, 2)), 3)

    def spectrum_rows(slot, e):
        return halves(spec[pl.ds(slot * 1024 + e, 128, stride=8), :])

    for e in range(8):
        back = (8 - e) % 8
        flip = flips[0 if e == 0 else 1]
        codes = []
        for s in range(SLOTS):
            h, l = spectrum_rows(own_slots[s], e)
            ear[s, e] = mm_t(own2[...], jnp.concatenate([h, l], axis=1))
            h, l = spectrum_rows(mir_slots[s], back)
            gh = mm_t(mir[...], h).astype(bf16)
            gl = mm_t(mir[...], l).astype(bf16)
            v = mm(jnp.concatenate([gh, gl], axis=1), flip)
            q = jnp.round((jnp.log(v) - SPEC_LOW) * SPEC_CODE - 32500.0)
            codes.append(jnp.clip(q, -32767.0, 32767.0))
        vs[e] = pack(codes[0], codes[1])

    v_main = pltpu.make_async_remote_copy(
        src_ref=vs, dst_ref=vr, send_sem=v_send.at[0], recv_sem=v_recv.at[0],
        device_id={"narrow": 7 - me_n}, device_id_type=MESH,
    )
    v_side = pltpu.make_async_remote_copy(
        src_ref=vs.at[:, pl.ds(0, 8), :], dst_ref=vc, send_sem=v_send.at[1], recv_sem=v_recv.at[1],
        device_id={"narrow": lax.rem(8 - me_n, 8)}, device_id_type=MESH,
    )
    v_main.start()
    alone = (me_n == 0) | (me_n == 4)

    @pl.when(jnp.logical_not(alone))
    def _():
        v_side.start()

    @pl.when(alone)
    def _():
        vc[...] = vs[:, 0:8, :]

    def second_forward(s, p, q, r):
        def group(g, _):
            dec = [decode_factor(wr[s, 4 * b + g, 32:40, :]) for b in range(8)]
            dec = [jnp.concatenate([d, d], axis=0) for d in dec]
            for t in range(2):
                v = []
                for b in range(8):
                    re, im = unpack(wr[s, 4 * b + g, 16 * t : 16 * t + 16, :])
                    re, im = re * dec[b], im * dec[b]
                    if p is not None:
                        re, im = re * p + im * q, im * r
                    v.append((re, im))
                v = dft8(v, -1)
                at = rows16(g * 32 + 16 * t, 16)
                at_im = rows16(128 + g * 32 + 16 * t, 16)
                for c in range(8):
                    w = v[c] if c == 0 else turn(v[c], tyc[c, at, :], tys[c, at, :], -1)
                    lanes = slice(128 * (c % 2), 128 * (c % 2) + 128)
                    for dst, part in ((at, w[0]), (at_im, w[1])):
                        h, l = halves(part)
                        bh[c // 2, dst, lanes] = h
                        bl[c // 2, dst, lanes] = l
            return 0

        lax.fori_loop(0, 4, group, 0)
        for cp in range(4):
            big[cp] = mm(yf[0], bh[cp]) + mm(yf[1], bh[cp]) + mm(yf[0], bl[cp])

    first_row = lax.broadcasted_iota(i32, (8, 128), 0) == 0

    def code_narrow(s, n):
        tiles = []
        for c in range(8):
            lanes = slice(128 * (c % 2), 128 * (c % 2) + 128)
            for t in range(2):
                tiles.append((
                    big[c // 2, rows(16 * n + 8 * t, 8), lanes],
                    big[c // 2, rows(128 + 16 * n + 8 * t, 8), lanes],
                ))
        code = scale_code(tile_max([x for pair in tiles for x in pair]))
        fac = encode_factor(code)
        for k, (re, im) in enumerate(tiles):
            ns[s, n, 8 * k : 8 * k + 8, :] = pack(re * fac, im * fac)
        ns[s, n, 128:136, :] = code

    for s in range(SLOTS):
        recv_all(wide_copy, WIDE, me_w, w_args, s)
        if s == 0:
            one = jnp.where(special, 0.0, 1.0)
            second_forward(s, 1.0, 0.0, one)

            @pl.when(special)
            def _():
                big2[...] = big[...]
                second_forward(0, 0.0, 1.0, 0.0)
                top = big[0, 0:8, 0:128]
                mid = big[0, 64:72, 0:128]
                big[:, 0:64, :] = big2[:, 0:64, :]
                big[:, 128:192, :] = big2[:, 128:192, :]
                big[0, 128:136, 0:128] = jnp.where(first_row, top, big[0, 128:136, 0:128])
                big[0, 192:200, 0:128] = jnp.where(first_row, mid, big[0, 192:200, 0:128])
                big[0, 64:72, 0:128] = jnp.where(first_row, big2[0, 64:72, 0:128], mid)
        else:
            second_forward(s, None, None, None)

        def code_n(n, _, s=s):
            code_narrow(s, n)
            return 0

        lax.fori_loop(0, NARROW, code_n, 0)
        nr[s, me_n] = ns[s, me_n]
        send_all(narrow_copy, NARROW, me_n, n_args, s)

    total = 1.0 / (NX * NY * NZ)
    v_main.wait_recv()

    @pl.when(jnp.logical_not(alone))
    def _():
        v_side.wait_recv()

    def decode_spectrum(q):
        return jnp.exp((q + 32500.0) * (1.0 / SPEC_CODE) + SPEC_LOW)

    bsp[...] = jnp.zeros_like(bsp)

    @pl.when(edge)
    def _():
        sigma = jnp.where(me_n == 0, 1.0, -1.0)
        xs, vv = [], []
        for e in range(8):
            xs.append(ear[0, e, 0:8, :])
            vv.append(decode_spectrum(unpack(vc[e])[0]))

        def even(list_of, e):
            h, l = halves(list_of[(8 - e) % 8])
            pair = jnp.concatenate([h, l], axis=1)
            flip = flips[0 if e == 0 else 1]
            return (mm(pair, flip) + list_of[e]) * 0.5

        for e in range(8):
            a, b = even(xs, e), even(vv, e)
            bsp[e, 0:8, :] = jnp.where(first_row, (a - b) * (0.5 * total) * sigma, 0.0)
            big2[0, 8 * e : 8 * e + 8, 0:128] = (a + b) * (0.5 * total)

    for e in range(8):
        m0, m1 = unpack(vr[e])
        s0, s1 = unpack(vc[e])
        for s, m, side in ((0, m0, s0), (1, m1, s1)):
            m, side = decode_spectrum(m), decode_spectrum(side)
            ear_e = ear[s, e]
            lead = jnp.where(first_row, side, m[0:8])
            ear[s, e, 8:128, :] = (ear_e[8:128] + m[8:128]) * (0.5 * total)
            ear[s, e, 0:8, :] = (ear_e[0:8] + lead) * (0.5 * total)

    @pl.when(edge)
    def _():
        for e in range(8):
            ear[0, e, 0:8, :] = jnp.where(
                first_row, big2[0, 8 * e : 8 * e + 8, 0:128], ear[0, e, 0:8, :]
            )

    def first_both(s):
        def decs(n):
            d = decode_factor(nr[s, n, 128:136, :])
            return jnp.concatenate([d, d], axis=0)

        for n in range(8):
            big2[0, 16 * n : 16 * n + 16, 0:128] = decs(n)

        def load(c):
            v = []
            for n in range(8):
                re, im = unpack(nr[s, n, rows16(16 * c, 16), :])
                d = big2[0, 16 * n : 16 * n + 16, 0:128]
                v.append((re * d, im * d))
            return v

        def put(v, at):
            v = dft8(v, -1)
            for e in range(8):
                w = v[e] if e == 0 else turn(v[e], tx[0, e : e + 1, :], tx[1, e : e + 1, :], -1)
                for lanes, part in ((slice(0, 128), w[0]), (slice(128, 256), w[1])):
                    h, l = halves(part)
                    lh[e, at, lanes] = h
                    ll[e, at, lanes] = l

        def block(c, _):
            put(load(c), rows16(16 * c, 16))
            return 0

        lax.fori_loop(0, 8, block, 0)
        if s == 0:
            put([(re, -im) for re, im in load(0)], slice(128, 144))
        count = 144 if s == 0 else 128
        for e in range(8):
            h, l = lh[e, 0:count, :], ll[e, 0:count, :]
            z = mm(h, xf[0]) + mm(h, xf[1]) + mm(l, xf[0])
            fil = jnp.concatenate([ear[s, e], ear[s, e]], axis=1)
            g = z[0:128] * fil
            if s == 0:
                extra = jnp.concatenate([bsp[e], bsp[e]], axis=1)
                g = jnp.concatenate([g[0:16] + z[128:144] * extra, g[16:128]], axis=0)
            h, l = halves(g)
            big[e // 2, 128 * (e % 2) : 128 * (e % 2) + 128, :] = (
                mm(h, xi[0]) + mm(h, xi[1]) + mm(l, xi[0])
            )

        def unblock(c, _):
            v = []
            for e in range(8):
                at = rows16(128 * (e % 2) + 16 * c, 16)
                y = (big[e // 2, at, 0:128], big[e // 2, at, 128:256])
                v.append(y if e == 0 else turn(y, tx[0, e : e + 1, :], tx[1, e : e + 1, :], 1))
            v = dft8(v, 1)
            for n in range(8):
                at = rows16(128 * (n % 2) + 16 * c, 16)
                big2[n // 2, at, 0:128] = v[n][0]
                big2[n // 2, at, 128:256] = v[n][1]
            return 0

        lax.fori_loop(0, 8, unblock, 0)
        for n in range(8):
            base = 128 * (n % 2)
            tiles = [
                (big2[n // 2, base + 8 * k : base + 8 * k + 8, 0:128],
                 big2[n // 2, base + 8 * k : base + 8 * k + 8, 128:256])
                for k in range(16)
            ]
            code = scale_code(tile_max([x for pair in tiles for x in pair]))
            fac = encode_factor(code)
            for k, (re, im) in enumerate(tiles):
                ms[s, n, 8 * k : 8 * k + 8, :] = pack(re * fac, im * fac)
            ms[s, n, 128:136, :] = code

    for s in range(SLOTS):
        recv_all(narrow_copy, NARROW, me_n, n_args, s)
        first_both(s)
        mr[s, me_n] = ms[s, me_n]
        send_all(narrow_copy, NARROW, me_n, m_args, s)

    row16 = lax.broadcasted_iota(i32, (16, 128), 0)

    def second_back(s, part):
        def fill(n, _):
            d = decode_factor(mr[s, n, 128:136, :])
            d = jnp.concatenate([d, d], axis=0)
            if part is not None:
                if part == 0:
                    f = jnp.where(special, jnp.where(n < 4, 2.0, 0.0), 1.0)
                else:
                    f = jnp.where(n < 4, 0.0, 2.0)
                hit = (row16 == 0) & (special & ((n == 0) | (n == 4)))
            for c in range(8):
                re, im = unpack(mr[s, n, 16 * c : 16 * c + 16, :])
                re, im = re * d, im * d
                if part == 0:
                    if c == 0:
                        re, im = jnp.where(hit, re, re * f), jnp.where(hit, 0.0, im * f)
                    else:
                        re, im = re * f, im * f
                elif part == 1:
                    if c == 0:
                        re, im = jnp.where(hit, im, re * f), jnp.where(hit, 0.0, im * f)
                    else:
                        re, im = re * f, im * f
                lanes = slice(128 * (c % 2), 128 * (c % 2) + 128)
                for dst, x in ((rows16(16 * n, 16), re), (rows16(128 + 16 * n, 16), im)):
                    h, l = halves(x)
                    bh[c // 2, dst, lanes] = h
                    bl[c // 2, dst, lanes] = l
            return 0

        lax.fori_loop(0, 8, fill, 0)
        for cp in range(4):
            big[cp] = mm(yi[0], bh[cp]) + mm(yi[1], bh[cp]) + mm(yi[0], bl[cp])

        def spread(t, _):
            v = []
            at = rows16(16 * t, 16)
            for c in range(8):
                lanes = slice(128 * (c % 2), 128 * (c % 2) + 128)
                y = (big[c // 2, at, lanes], big[c // 2, rows16(128 + 16 * t, 16), lanes])
                v.append(y if c == 0 else turn(y, tyc[c, at, :], tys[c, at, :], 1))
            v = dft8(v, 1)
            for b in range(8):
                to = rows16(128 * (b % 2) + 16 * t, 16)
                if part == 1:
                    big2[b // 2, to, 128:256] = v[b][0]
                else:
                    big2[b // 2, to, 0:128] = v[b][0]
                    big2[b // 2, to, 128:256] = v[b][1]
            return 0

        lax.fori_loop(0, 8, spread, 0)

    for s in range(SLOTS):
        recv_all(narrow_copy, NARROW, me_n, m_args, s)
        second_back(s, 0 if s == 0 else None)
        if s == 0:
            @pl.when(special)
            def _():
                second_back(0, 1)

        def read_back(w):
            b = w // 4
            at = rows((b % 2) * 128 + (w % 4) * 32, 32)
            return big2[b // 2, at, 0:128], big2[b // 2, at, 128:256]

        def code_back(w, _, s=s):
            code_wide(read_back, us, s, w, w)
            return 0

        lax.fori_loop(0, WIDE, code_back, 0)
        keep = pltpu.make_async_copy(us.at[s, me_w], out.at[s, me_w], u_recv.at[s, me_w])
        keep.start()
        send_all(wide_copy, WIDE, me_w, u_args, s)

    for s in range(SLOTS):
        pltpu.make_async_copy(us.at[s, me_w], out.at[s, me_w], u_recv.at[s, me_w]).wait()
        recv_all(wide_copy, WIDE, me_w, u_args, s)
        sent_all(wide_copy, WIDE, me_w, w_args, s)
        sent_all(narrow_copy, NARROW, me_n, n_args, s)
        sent_all(narrow_copy, NARROW, me_n, m_args, s)
        sent_all(wide_copy, WIDE, me_w, u_args, s)
    v_main.wait_send()

    @pl.when(jnp.logical_not(alone))
    def _():
        v_side.wait_send()


def spectral(noise, spectrum):
    t = TABLES
    angle = 2 * np.pi * np.arange(8)[:, None] * np.arange(128)[None, :] / 1024
    tyc = jnp.broadcast_to(jnp.asarray(np.cos(angle), f32)[:, :, None], (8, 128, 128))
    tys = jnp.broadcast_to(jnp.asarray(np.sin(angle), f32)[:, :, None], (8, 128, 128))
    vmem = pl.BlockSpec(memory_space=pltpu.VMEM)
    dma = pltpu.SemaphoreType.DMA
    return pl.pallas_call(
        spectral_kernel,
        out_shape=jax.ShapeDtypeStruct((SLOTS, WIDE, 40, 128), i32),
        in_specs=[vmem] * 13,
        out_specs=pl.BlockSpec(memory_space=pl.ANY),
        scratch_shapes=[
            pltpu.VMEM((2048, 128), f32),
            pltpu.VMEM((2048, 128), f32),
            pltpu.VMEM((SLOTS, WIDE, 40, 128), i32),
            pltpu.VMEM((SLOTS, WIDE, 40, 128), i32),
            pltpu.VMEM((4, 256, 256), bf16),
            pltpu.VMEM((4, 256, 256), bf16),
            pltpu.VMEM((4, 256, 256), f32),
            pltpu.VMEM((4, 256, 256), f32),
            pltpu.VMEM((SLOTS, NARROW, 136, 128), i32),
            pltpu.VMEM((SLOTS, NARROW, 136, 128), i32),
            pltpu.VMEM((8, 144, 256), bf16),
            pltpu.VMEM((8, 144, 256), bf16),
            pltpu.VMEM((SLOTS, NARROW, 136, 128), i32),
            pltpu.VMEM((SLOTS, NARROW, 136, 128), i32),
            pltpu.VMEM((SLOTS, WIDE, 40, 128), i32),
            pltpu.VMEM((SLOTS, 8, 128, 128), f32),
            pltpu.VMEM((8, 16, 128), f32),
            pltpu.VMEM((8, 128, 128), i32),
            pltpu.VMEM((8, 128, 128), i32),
            pltpu.VMEM((8, 8, 128), i32),
            dma((SLOTS, WIDE)), dma((SLOTS, WIDE)),
            dma((SLOTS, NARROW)), dma((SLOTS, NARROW)),
            dma((SLOTS, NARROW)), dma((SLOTS, NARROW)),
            dma((SLOTS, WIDE)), dma((SLOTS, WIDE)),
            dma((2,)), dma((2,)),
        ],
        compiler_params=pltpu.CompilerParams(
            collective_id=0, has_side_effects=True, vmem_limit_bytes=56 * 1024 * 1024
        ),
    )(
        noise.reshape(4096, 128), spectrum.reshape(4096, 128), t["tz"], t["yf"], t["yi"],
        t["xf"], t["xi"], tyc, tys, t["tx"], t["own2"], t["mir"], t["flips"],
    )


def finish_kernel(
    cell_row, target, freq, tzi, depth_at, assay, weight, out,
    got, contrib, *accs,
):
    for acc in accs:
        acc[...] = jnp.zeros_like(acc)

    def depth(y, _):
        re, im = unpack(freq[pl.ds(y, 64, stride=40), :])
        d = decode_factor(freq[pl.ds(32 + lax.rem(y, 8), 64, stride=40), :])
        h, l = halves(jnp.concatenate([re * d, im * d], axis=0))
        u = jnp.concatenate([h, h, l], axis=0)
        out[pl.ds(y, 128, stride=32), :] = lax.dot_general(
            u, tzi[...], (((0,), (0,)), ((), ())), preferred_element_type=f32
        )
        return 0

    lax.fori_loop(0, 32, depth, 0)
    count = got.shape[0]

    def gather(g, _):
        for k in range(16):
            i = g * 16 + k
            got[pl.ds(i, 1), :] = out[pl.ds(cell_row[i], 1), :]
        return 0

    lax.fori_loop(0, count // 16, gather, 0)
    lane = lax.broadcasted_iota(i32, (128, 128), 1)

    def residual(g, _):
        at = rows16(g * 128, 128)
        value = jnp.sum(jnp.where(lane == depth_at[at, :], got[at, :], 0.0), axis=1, keepdims=True)
        resid = assay[at, :] - value
        for k in range(TARGETS):
            contrib[k, at, :] = resid * weight[at, 128 * k : 128 * k + 128].astype(f32)
        return 0

    lax.fori_loop(0, count // 128, residual, 0)

    def scatter(g, _):
        for k in range(4):
            i = g * 4 + k
            for t in range(TARGETS):
                acc = accs[t + TARGETS * (k % 2)]
                at = pl.ds(target[i * TARGETS + t], 1)
                acc[at, :] = acc[at, :] + contrib[t, pl.ds(i, 1), :]
        return 0

    lax.fori_loop(0, count // 4, scatter, 0)

    def combine(g, _):
        at = rows(g * 64, 64)
        v = out[at, :]
        for acc in accs:
            v = v + acc[at, :]
        out[at, :] = v
        return 0

    lax.fori_loop(0, 64, combine, 0)


def finish(freq, cell, target, assay, weight):
    vmem = pl.BlockSpec(memory_space=pltpu.VMEM)
    smem = pl.BlockSpec(memory_space=pltpu.SMEM)
    count = cell.shape[0]
    return pl.pallas_call(
        finish_kernel,
        out_shape=jax.ShapeDtypeStruct((4096, 128), f32),
        in_specs=[smem, smem] + [vmem] * 5,
        out_specs=vmem,
        scratch_shapes=[pltpu.VMEM((count, 128), f32), pltpu.VMEM((TARGETS, count, 128), f32)]
        + [pltpu.VMEM((4096, 128), f32)] * 8,
        compiler_params=pltpu.CompilerParams(vmem_limit_bytes=56 * 1024 * 1024),
    )(
        cell // NZ, target.reshape(-1), freq.reshape(-1, 128), TABLES["tzi"],
        (cell % NZ)[:, None], assay[:, None], weight,
    )


def deliver(assay, weights, owner, cell, pencils):
    count = owner.shape[0]
    capacity = max(4, 4 * count // (WIDE * NARROW))
    order = jnp.arange(count, dtype=i32)
    earlier = (order[None, :] < order[:, None]) & (owner[None, :] == owner[:, None])
    slot = owner * capacity + jnp.sum(earlier, axis=1, dtype=i32)
    total = WIDE * NARROW * capacity
    hot = jnp.arange(total, dtype=i32)[:, None] == slot[None, :]
    placed = jnp.dot(hot.astype(bf16), weights, preferred_element_type=bf16)
    fields = jnp.concatenate(
        [cell[None], pencils.T, jnp.zeros((3, count), i32)], axis=0
    ).astype(f32)
    numbers = lax.dot_general(
        fields, hot.astype(f32), (((1,), (1,)), ((), ())), precision=lax.Precision.HIGHEST
    )
    numbers = jnp.round(numbers).astype(i32)
    grade = jnp.sum(jnp.where(hot, assay.astype(f32)[None, :], 0.0), axis=1).astype(bf16)

    def both(x):
        x = lax.all_to_all(x, "wide", split_axis=0, concat_axis=0, tiled=True)
        return lax.all_to_all(x, "narrow", split_axis=1, concat_axis=1, tiled=True)

    placed = both(placed.reshape(WIDE, NARROW, capacity, TARGETS * NZ)).reshape(total, TARGETS * NZ)
    numbers = numbers.reshape(8, WIDE, NARROW, capacity).transpose(1, 2, 0, 3)
    numbers = both(numbers.reshape(WIDE, NARROW, 8 * capacity))
    numbers = numbers.reshape(WIDE * NARROW, 8, capacity).transpose(1, 0, 2).reshape(8, total)
    grade = both(grade.reshape(WIDE, NARROW, capacity)).reshape(total)
    return numbers[0], numbers[1 : 1 + TARGETS].T, grade.astype(f32), placed


def local(noise, spectrum, assay, measure_weights, measure_owner, measure_cell, measure_pencils):
    count = measure_owner.shape[1]
    cell, target, grade, placed = deliver(
        assay[0], measure_weights[0].reshape(count, TARGETS * NZ), measure_owner[0],
        measure_cell[0], measure_pencils[0],
    )
    freq = spectral(noise, spectrum)
    field = finish(freq, cell, target, grade, placed)
    return field.reshape(noise.shape)


def solution(mesh):
    placed = (
        P("narrow", "wide", None),
        P("wide", None, "narrow"),
        P(("wide", "narrow"), None),
        P(("wide", "narrow"), None, None, None),
        P(("wide", "narrow"), None),
        P(("wide", "narrow"), None),
        P(("wide", "narrow"), None, None),
    )
    return jax.shard_map(
        local, mesh=mesh, in_specs=placed, out_specs=P("narrow", "wide", None), check_vma=False
    )
```

time: 610 us -> 276 us (0.45); the launches traced: 598 us -> 274 us
  local copies, waits for them, and re-layouts: 208 us -> 19.8 us
  Pallas kernels: 0 us -> 166 us
  waiting for transfers between devices: 181 us -> 41.2 us
  other arithmetic: 81.2 us -> 6.31 us
  matrix products: 53.3 us -> 5.18 us
  starting transfers between devices: 74.6 us -> 35.7 us
    pallas_call x0 -> x2, Pallas kernels: none -> 166 us  [the longest x1 135 us: spectral(): pl.pallas_call(spectral_kernel, out_shape=jax.ShapeDtypeStruct((SLOTS, WI...]
    all_to_all x10 -> x6, waiting for transfers between devices: 181 us -> 41.2 us  [the longest x3 35.4 us: both(): x = lax.all_to_all(x, 'wide', split_axis=0, concat_axis=0, tiled=True)]
    scatter x5 -> x0, local copies, waits for them, and re-layouts: 118 us -> none  [the longest x1 58.1 us: local(): weight_holder.at[wide_target, narrow_target, slot_position]]
    scatter-add x1 -> x0, other arithmetic: 59.1 us -> none  [local(): jnp.zeros((size_x * size_y, depth), jnp.float32).at[targets]]
    dot_general x10 -> x2, matrix products: 53.3 us -> 5.18 us  [the longest x1 2.67 us: deliver(): lax.dot_general(fields, hot.astype(f32), (((1,), (1,)), ((), ())), precis...]
    all_to_all x10 -> x6, starting transfers between devices: 74.6 us -> 35.7 us  [the longest x3 18.6 us: both(): return lax.all_to_all(x, 'narrow', split_axis=1, concat_axis=1, tiled=True)]
    transpose x7 -> x2, local copies, waits for them, and re-layouts: 21 us -> 1.72 us  [the longest x1 1.34 us: deliver(): return (numbers[0], numbers[1:1 + TARGETS].T, grade.astype(f32), placed)]
    all_to_all x10 -> x6, local copies, waits for them, and re-layouts: 22.7 us -> 4.7 us  [the longest x2 2.55 us: both(): return lax.all_to_all(x, 'narrow', split_axis=1, concat_axis=1, tiled=True)]
  transfers between devices with their start and end apart: 10 -> 6, of which waited for: 4 -> 5; matrix products, arithmetic and copies ran while one was open for 40% -> 9% of each run, Pallas kernels for 0% -> 49%
where the time goes in v1:
time: 276 us; the launch traced here: 274 us
  Pallas kernels  166 us (60%)
  waiting for transfers between devices  41.2 us (15%)
  starting transfers between devices  35.7 us (13%)
  local copies, waits for them, and re-layouts  19.8 us (7%)
  other arithmetic  6.31 us (2%)
  matrix products  5.18 us (2%)
    pallas_call x1, Pallas kernels, spectral(): pl.pallas_call(spectral_kernel, out_shape=jax.ShapeDtypeStruct((SLOTS, WI...  135 us
    all_to_all x3, waiting for transfers between devices, both(): x = lax.all_to_all(x, 'wide', split_axis=0, concat_axis=0, tiled=True)  35.4 us
    pallas_call x1, Pallas kernels, finish(): pl.pallas_call(finish_kernel, out_shape=jax.ShapeDtypeStruct((4096, 128),...  30.4 us
    all_to_all x3, starting transfers between devices, both(): return lax.all_to_all(x, 'narrow', split_axis=1, concat_axis=1, tiled=True)  18.6 us
    all_to_all x3, starting transfers between devices, both(): x = lax.all_to_all(x, 'wide', split_axis=0, concat_axis=0, tiled=True)  17.1 us
    all_to_all x3, waiting for transfers between devices, both(): return lax.all_to_all(x, 'narrow', split_axis=1, concat_axis=1, tiled=True)  5.85 us
  transfers between devices with their start and end apart: 6, of which 5 were waited for; matrix products, arithmetic and copies ran while one was open for 9% of the time, Pallas kernels for 49%

profile of v1, /device:TPU:65, one launch (start us, length us, event | category | flops | bytes accessed | tf_op | source)
XLA Modules:
  0.0 274.1 jit_solution(14261285474220778406)
XLA Ops:
  0.0 1.0 convert_reduce_fusion
  3.7 7.8 %all-to-all-start.2 = ((bf16[32,8,8]{2,1,0:T(8,128)(2,1)}), bf16[32,8,8]{2,1,0:T(8,128)(2,1)S(1)}, u32[]{:S(2)}, u32[]{:S(2)}) async-start(bf16[32,8,8]{2,1,0:T(8,128)(2,1)} %convert_element_type.37), calls=%async_computation.2 | async-start | bytes 131072 | tf_op jit(solution)/shard_map/all_to_all | solution.py:765
  11.5 2.7 fusion.4
  14.2 4.6 %all-to-all-done.2 = bf16[32,8,8]{2,1,0:T(8,128)(2,1)S(1)} async-done(((bf16[32,8,8]{2,1,0:T(8,128)(2,1)}), bf16[32,8,8]{2,1,0:T(8,128)(2,1)S(1)}, u32[]{:S(2)}, u32[]{:S(2)}) %all-to-all-start.2) | async-done | bytes 4128 | tf_op jit(solution)/shard_map/all_to_all | solution.py:765
  19.5 7.6 %all-to-all-start.3 = ((bf16[8,2,128]{2,1,0:T(2,128)(2,1)}), bf16[8,2,128]{2,1,0:T(2,128)(2,1)S(1)}, u32[]{:S(2)}, u32[]{:S(2)}) async-start(bf16[8,2,128]{2,1,0:T(2,128)(2,1)} %reshape.140), calls=%async_computation.3 | async-start | bytes 8192 | tf_op jit(solution)/shard_map/all_to_all | solution.py:766
  29.2 2.3 all-to-all-done.3
  31.5 5.3 %all-to-all-start = ((s32[32,1,512]{2,1,0:T(1,128)}), s32[32,1,512]{2,1,0:T(1,128)S(1)}, u32[]{:S(2)}, u32[]{:S(2)}) async-start(s32[32,1,512]{2,1,0:T(1,128)} %reshape.142), calls=%async_computation | async-start | bytes 131072 | tf_op jit(solution)/shard_map/all_to_all | solution.py:765
  36.8 2.5 fusion.1
  39.3 4.9 %all-to-all-done = s32[32,1,512]{2,1,0:T(1,128)S(1)} async-done(((s32[32,1,512]{2,1,0:T(1,128)}), s32[32,1,512]{2,1,0:T(1,128)S(1)}, u32[]{:S(2)}, u32[]{:S(2)}) %all-to-all-start) | async-done | bytes 65568 | tf_op jit(solution)/shard_map/all_to_all | solution.py:765
  44.2 4.1 %all-to-all-start.4 = ((bf16[32,8,8,512]{3,2,1,0:T(8,128)(2,1)}), bf16[32,8,8,512]{3,2,1,0:T(8,128)(2,1)S(1)}, u32[]{:S(2)}, u32[]{:S(2)}) async-start(bf16[32,8,8,512]{3,2,1,0:T(8,128)(2,1)} %fusion.1), calls=%async_computation.4 | async-start | bytes 4194304 | tf_op jit(solution)/shard_map/all_to_all | solution.py:765
  50.4 25.9 %all-to-all-done.4 = bf16[32,8,8,512]{3,2,1,0:T(8,128)(2,1)S(1)} async-done(((bf16[32,8,8,512]{3,2,1,0:T(8,128)(2,1)}), bf16[32,8,8,512]{3,2,1,0:T(8,128)(2,1)S(1)}, u32[]{:S(2)}, u32[]{:S(2)}) %all-to-all-start.4) | async-done | bytes 2097184 | tf_op jit(solution)/shard_map/all_to_all | solution.py:765
  76.2 5.3 %all-to-all-start.1 = ((s32[8,1,2048]{2,1,0:T(1,128)}), s32[8,1,2048]{2,1,0:T(1,128)S(1)}, u32[]{:S(2)}, u32[]{:S(2)}) async-start(s32[8,1,2048]{2,1,0:T(1,128)} %reshape.144), calls=%async_computation.1 | async-start | bytes 131072 | tf_op jit(solution)/shard_map/all_to_all | solution.py:766
  81.6 1.5 copy.59
  83.1 3.6 %all-to-all-done.1 = s32[8,1,2048]{2,1,0:T(1,128)S(1)} async-done(((s32[8,1,2048]{2,1,0:T(1,128)}), s32[8,1,2048]{2,1,0:T(1,128)S(1)}, u32[]{:S(2)}, u32[]{:S(2)}) %all-to-all-start.1) | async-done | bytes 65568 | tf_op jit(solution)/shard_map/all_to_all | solution.py:766
  86.7 5.7 %all-to-all-start.5 = ((bf16[32,8,8,512]{3,2,0,1:T(8,128)(2,1)}), bf16[32,8,8,512]{3,2,0,1:T(8,128)(2,1)S(1)}, u32[]{:S(2)}, u32[]{:S(2)}) async-start(bf16[32,8,8,512]{3,2,0,1:T(8,128)(2,1)} %copy.59), calls=%async_computation.5 | async-start | bytes 4194304 | tf_op jit(solution)/shard_map/all_to_all | solution.py:766
  94.3 135.3 %shard_map.181 = s32[2,32,40,128]{3,2,1,0:T(8,128)} custom-call(f32[4096,128]{1,0:T(8,128)} %bitcast.30, f32[4096,128]{1,0:T(8,128)} %bitcast.31, bf16[128,384]{1,0:T(8,128)(2,1)} %constant.59.clone.tz, bf16[2,256,256]{2,1,0:T(8,128)(2,1)} %constant.60.clone.yf.xi, bf16[2,256,256]{2,1,0:T(8,128)(2,1)} %constant.61.clone.yi.xf, ...), custom_call_target="tpu_custom_call" | custom-call | tf_op jit(solution)/shard_map/pallas_call | solution.py:626
  229.9 1.3 reshape.138.assay
  234.0 1.0 copy.51
  235.0 1.3 slice.12
  236.4 1.3 copy.52
  237.7 2.4 reshape.129.target
  240.7 1.3 add_select_fusion.depth_at
  242.1 1.6 copy.60
  243.7 30.4 %shard_map.182 = f32[4096,128]{1,0:T(8,128)} custom-call(s32[2048]{0:T(1024)} %add_select_fusion.1.cell_row, s32[8192]{0:T(1024)} %reshape.129.target, s32[2560,128]{1,0:T(8,128)} %bitcast.28, bf16[384,128]{1,0:T(8,128)(2,1)} %constant.66.clone.tzi, s32[2048,1]{1,0:T(8,128)} %add_select_fusion.depth_at, f32[2048,1]{1,0:T(8,128)} %reshape.138.assay, ...), custom_call_target="tpu_custom_call" | custom-call | tf_op jit(solution)/shard_map/pallas_call | solution.py:732
  (40 shorter events, 13.3 us)
Async XLA Ops:
  3.7 15.1 %all-to-all-start.2 = ((bf16[32,8,8]{2,1,0:T(8,128)(2,1)}), bf16[32,8,8]{2,1,0:T(8,128)(2,1)S(1)}, u32[]{:S(2)}, u32[]{:S(2)}) async-start(bf16[32,8,8]{2,1,0:T(8,128)(2,1)} %convert_element_type.37), calls=%async_computation.2 | async-start | bytes 131072 | tf_op jit(solution)/shard_map/all_to_all | solution.py:765
  11.5 17.5 %copy-start = (bf16[1,512,4,128]{3,2,1,0:T(4,128)(2,1)S(1)}, bf16[1,512,4,128]{3,2,1,0:T(4,128)(2,1)}, u32[]{:S(2)}) copy-start(bf16[1,512,4,128]{3,2,1,0:T(4,128)(2,1)} %param.22) | copy-start | bytes 1572868
  19.5 11.9 %all-to-all-start.3 = ((bf16[8,2,128]{2,1,0:T(2,128)(2,1)}), bf16[8,2,128]{2,1,0:T(2,128)(2,1)S(1)}, u32[]{:S(2)}, u32[]{:S(2)}) async-start(bf16[8,2,128]{2,1,0:T(2,128)(2,1)} %reshape.140), calls=%async_computation.3 | async-start | bytes 8192 | tf_op jit(solution)/shard_map/all_to_all | solution.py:766
  31.5 12.7 %all-to-all-start = ((s32[32,1,512]{2,1,0:T(1,128)}), s32[32,1,512]{2,1,0:T(1,128)S(1)}, u32[]{:S(2)}, u32[]{:S(2)}) async-start(s32[32,1,512]{2,1,0:T(1,128)} %reshape.142), calls=%async_computation | async-start | bytes 131072 | tf_op jit(solution)/shard_map/all_to_all | solution.py:765
  44.2 32.0 %all-to-all-start.4 = ((bf16[32,8,8,512]{3,2,1,0:T(8,128)(2,1)}), bf16[32,8,8,512]{3,2,1,0:T(8,128)(2,1)S(1)}, u32[]{:S(2)}, u32[]{:S(2)}) async-start(bf16[32,8,8,512]{3,2,1,0:T(8,128)(2,1)} %fusion.1), calls=%async_computation.4 | async-start | bytes 4194304 | tf_op jit(solution)/shard_map/all_to_all | solution.py:765
  76.2 10.4 %all-to-all-start.1 = ((s32[8,1,2048]{2,1,0:T(1,128)}), s32[8,1,2048]{2,1,0:T(1,128)S(1)}, u32[]{:S(2)}, u32[]{:S(2)}) async-start(s32[8,1,2048]{2,1,0:T(1,128)} %reshape.144), calls=%async_computation.1 | async-start | bytes 131072 | tf_op jit(solution)/shard_map/all_to_all | solution.py:766
  83.1 9.2 %copy-start.2 = (f32[8,128]{1,0:T(8,128)S(1)}, f32[8,128]{1,0:T(8,128)}, u32[]{:S(2)}) copy-start(f32[8,128]{1,0:T(8,128)} %constant.57.clone) | copy-start | bytes 12292
  83.1 10.2 %copy-start.1 = (f32[8,128]{1,0:T(8,128)S(1)}, f32[8,128]{1,0:T(8,128)}, u32[]{:S(2)}) copy-start(f32[8,128]{1,0:T(8,128)} %constant.58.clone) | copy-start | bytes 12292
  86.7 155.4 %all-to-all-start.5 = ((bf16[32,8,8,512]{3,2,0,1:T(8,128)(2,1)}), bf16[32,8,8,512]{3,2,0,1:T(8,128)(2,1)S(1)}, u32[]{:S(2)}, u32[]{:S(2)}) async-start(bf16[32,8,8,512]{3,2,0,1:T(8,128)(2,1)} %copy.59), calls=%async_computation.5 | async-start | bytes 4194304 | tf_op jit(solution)/shard_map/all_to_all | solution.py:766

commit v2 on v1

--- a/solution.py
+++ b/solution.py
@@ -89,6 +89,18 @@
 
 
 TABLES = make_tables()
+ROOM = 256
+
+
+def join_matrix():
+    m = np.zeros((8, 128))
+    m[0, 1], m[0, 2] = 256, 1
+    for k in range(TARGETS):
+        m[1 + k, 4 + 2 * k], m[1 + k, 5 + 2 * k] = 256, 1
+    return m.astype(ml_dtypes.bfloat16)
+
+
+JOIN = join_matrix()
 
 
 def halves(v):
@@ -182,11 +194,12 @@
 
 
 def spectral_kernel(
-    noise, spec, tz, yf, yi, xf, xi, tyc, tys, tx, own2, mir, flips,
-    out,
+    noise, spec, tz, yf, yi, xf, xi, tyc, tys, tx, own2, mir, flips, place, parts, weights, join,
+    out, got, numbers,
     zre, zim, ws, wr, bh, bl, big, big2, ns, nr, lh, ll, ms, mr, us,
-    ear, bsp, vs, vr, vc,
+    ear, bsp, vs, vr, vc, asend, arecv, psend, precv, bsend, brecv,
     w_send, w_recv, n_send, n_recv, m_send, m_recv, u_send, u_recv, v_send, v_recv,
+    a_send, a_recv, p_send, p_recv, b_send, b_recv, g_sem,
 ):
     me_w = lax.axis_index("wide")
     me_n = lax.axis_index("narrow")
@@ -249,40 +262,6 @@
     n_args = (ns, nr, n_send, n_recv)
     m_args = (ms, mr, m_send, m_recv)
     u_args = (us, out, u_send, u_recv)
-
-    def depth(y, _):
-        h, l = halves(noise[pl.ds(y, 128, stride=32), :])
-        res = mm_t(tz[...], jnp.concatenate([h, h, l], axis=1))
-        zre[pl.ds(y, 64, stride=32), :] = res[:64]
-        zim[pl.ds(y, 64, stride=32), :] = res[64:]
-        return 0
-
-    lax.fori_loop(0, 32, depth, 0)
-
-    def code_wide(read, dst, s, w, to):
-        re, im = read(w)
-        m = tile_max([re[8 * t : 8 * t + 8] for t in range(4)] + [im[8 * t : 8 * t + 8] for t in range(4)])
-        code = scale_code(m)
-        fac = encode_factor(code)
-        for t in range(4):
-            sl = slice(8 * t, 8 * t + 8)
-            dst[s, to, 8 * t : 8 * t + 8, :] = pack(re[sl] * fac, im[sl] * fac)
-        dst[s, to, 32:40, :] = code
-
-    for s in range(SLOTS):
-        def read_depth(w, s=s):
-            at = rows((s * 32 + w) * 32, 32)
-            return zre[at, :], zim[at, :]
-
-        def code_one(w, _, s=s, read=read_depth):
-            code_wide(read, ws, s, w, w)
-            return 0
-
-        lax.fori_loop(0, WIDE, code_one, 0)
-        wr[s, me_w] = ws[s, me_w]
-        if s == 0:
-            pl.semaphore_wait(barrier, WIDE - 1 + NARROW - 1)
-        send_all(wide_copy, WIDE, me_w, w_args, s)
 
     late = special & (me_n >= 4)
     own_slots = (jnp.where(late, 2, 0), 1)
@@ -314,16 +293,120 @@
         src_ref=vs.at[:, pl.ds(0, 8), :], dst_ref=vc, send_sem=v_send.at[1], recv_sem=v_recv.at[1],
         device_id={"narrow": lax.rem(8 - me_n, 8)}, device_id_type=MESH,
     )
-    v_main.start()
+
     alone = (me_n == 0) | (me_n == 4)
-
-    @pl.when(jnp.logical_not(alone))
-    def _():
-        v_side.start()
 
     @pl.when(alone)
     def _():
         vc[...] = vs[:, 0:8, :]
+
+    room = asend.shape[1]
+    count = place.shape[1]
+    room_row = lax.broadcasted_iota(i32, (room, count), 0)
+
+    def pack_measures(n, _):
+        hot = jnp.where(room_row + n * room == place[...], 1.0, 0.0).astype(bf16)
+        asend[n] = mm(hot, weights[...]).astype(bf16)
+        psend[n] = mm_t(parts[...], hot).astype(bf16)
+        return 0
+
+    lax.fori_loop(0, NARROW, pack_measures, 0)
+    arecv[me_n] = asend[me_n]
+    precv[me_n] = psend[me_n]
+
+    def to_narrow(src, dst, sends, recvs, peer, slot):
+        return pltpu.make_async_remote_copy(
+            src_ref=src.at[peer], dst_ref=dst.at[slot], send_sem=sends.at[peer],
+            recv_sem=recvs.at[slot], device_id={"narrow": peer}, device_id_type=MESH,
+        )
+
+    def to_wide(peer, slot):
+        return pltpu.make_async_remote_copy(
+            src_ref=bsend.at[peer], dst_ref=brecv.at[slot], send_sem=b_send.at[peer],
+            recv_sem=b_recv.at[slot], device_id={"wide": peer}, device_id_type=MESH,
+        )
+
+    a_args = (asend, arecv, a_send, a_recv)
+    p_args = (psend, precv, p_send, p_recv)
+
+    def send_measures(i, _):
+        peer = lax.rem(me_n + i, NARROW)
+        to_narrow(*p_args, peer, me_n).start()
+        to_narrow(*a_args, peer, me_n).start()
+        return 0
+
+    def recv_measures(i, _):
+        peer = lax.rem(me_n + i, NARROW)
+        to_narrow(*p_args, peer, peer).wait_recv()
+        to_narrow(*a_args, peer, peer).wait_recv()
+        return 0
+
+    def sent_measures(i, _):
+        peer = lax.rem(me_n + i, NARROW)
+        to_narrow(*p_args, peer, peer).wait_send()
+        to_narrow(*a_args, peer, peer).wait_send()
+        return 0
+
+    def send_groups(i, _):
+        to_wide(lax.rem(me_w + i, WIDE), me_w).start()
+        return 0
+
+    def recv_groups(i, _):
+        peer = lax.rem(me_w + i, WIDE)
+        to_wide(peer, peer).wait_recv()
+        return 0
+
+    def sent_groups(i, _):
+        peer = lax.rem(me_w + i, WIDE)
+        to_wide(peer, peer).wait_send()
+        return 0
+
+    def depth(y, _):
+        cells = [y * 4 + k for k in range(4)]
+        pieces = []
+        for k in cells:
+            h, l = halves(noise[pl.ds(k, 128, stride=32), :])
+            pieces.append(jnp.concatenate([h, h, l], axis=1))
+        res = mm_t(tz[...], jnp.concatenate(pieces, axis=0))
+        for i, k in enumerate(cells):
+            zre[pl.ds(k, 64, stride=32), :] = res[:64, 128 * i : 128 * i + 128]
+            zim[pl.ds(k, 64, stride=32), :] = res[64:, 128 * i : 128 * i + 128]
+        return 0
+
+    lax.fori_loop(0, 8, depth, 0)
+
+    def code_wide(read, dst, s, w, to):
+        re, im = read(w)
+        m = tile_max([re[8 * t : 8 * t + 8] for t in range(4)] + [im[8 * t : 8 * t + 8] for t in range(4)])
+        code = scale_code(m)
+        fac = encode_factor(code)
+        for t in range(4):
+            sl = slice(8 * t, 8 * t + 8)
+            dst[s, to, 8 * t : 8 * t + 8, :] = pack(re[sl] * fac, im[sl] * fac)
+        dst[s, to, 32:40, :] = code
+
+    for s in range(SLOTS):
+        def read_depth(w, s=s):
+            at = rows((s * 32 + w) * 32, 32)
+            return zre[at, :], zim[at, :]
+
+        def code_one(w, _, s=s, read=read_depth):
+            code_wide(read, ws, s, w, w)
+            return 0
+
+        lax.fori_loop(0, WIDE, code_one, 0)
+        wr[s, me_w] = ws[s, me_w]
+        if s == 0:
+            pl.semaphore_wait(barrier, WIDE - 1 + NARROW - 1)
+        send_all(wide_copy, WIDE, me_w, w_args, s)
+        if s == 0:
+            v_main.start()
+
+            @pl.when(jnp.logical_not(alone))
+            def _():
+                v_side.start()
+
+            lax.fori_loop(1, NARROW, send_measures, 0)
 
     def second_forward(s, p, q, r):
         def group(g, _):
@@ -397,6 +480,27 @@
         lax.fori_loop(0, NARROW, code_n, 0)
         nr[s, me_n] = ns[s, me_n]
         send_all(narrow_copy, NARROW, me_n, n_args, s)
+
+
+    lax.fori_loop(1, NARROW, recv_measures, 0)
+    row = lax.broadcasted_iota(i32, (512, room), 0)
+    want = (((row >> 4) << 3) + (row & 7) + 1).astype(f32)
+    for q in range(4):
+        hot = []
+        for k in range(2):
+            key = precv[2 * q + k, 0:1, :].astype(f32)
+            match = (((row >> 3) & 1) == k) & (want == key)
+            hot.append(jnp.where(match, 1.0, 0.0).astype(bf16))
+        hot = jnp.concatenate(hot, axis=1)
+        held = jnp.concatenate([arecv[2 * q], arecv[2 * q + 1]], axis=0)
+        names = jnp.concatenate([precv[2 * q], precv[2 * q + 1]], axis=1)
+        moved = mm(hot, held).astype(bf16).reshape(WIDE, 16, 512)
+        named = mm_t(hot, names)
+        named = jnp.concatenate([named, jnp.zeros((512, 112), f32)], axis=1)
+        bsend[:, 16 * q : 16 * q + 16, 0:512] = moved
+        bsend[:, 16 * q : 16 * q + 16, 512:640] = named.astype(bf16).reshape(WIDE, 16, 128)
+    brecv[me_w] = bsend[me_w]
+    lax.fori_loop(1, WIDE, send_groups, 0)
 
     total = 1.0 / (NX * NY * NZ)
     v_main.wait_recv()
@@ -602,6 +706,17 @@
         keep.start()
         send_all(wide_copy, WIDE, me_w, u_args, s)
 
+    lax.fori_loop(1, WIDE, recv_groups, 0)
+    pltpu.make_async_copy(brecv, got, g_sem.at[0]).start()
+    for g in range(16):
+        named = jnp.concatenate(
+            [brecv[2 * g, :, 512:640], brecv[2 * g + 1, :, 512:640]], axis=0
+        )
+        numbers[g] = jnp.round(mm_t(join[...], named)).astype(i32)
+    lax.fori_loop(1, WIDE, sent_groups, 0)
+    lax.fori_loop(1, NARROW, sent_measures, 0)
+    pltpu.make_async_copy(brecv, got, g_sem.at[0]).wait()
+
     for s in range(SLOTS):
         pltpu.make_async_copy(us.at[s, me_w], out.at[s, me_w], u_recv.at[s, me_w]).wait()
         recv_all(wide_copy, WIDE, me_w, u_args, s)
@@ -616,7 +731,7 @@
         v_side.wait_send()
 
 
-def spectral(noise, spectrum):
+def spectral(noise, spectrum, place, parts, weights):
     t = TABLES
     angle = 2 * np.pi * np.arange(8)[:, None] * np.arange(128)[None, :] / 1024
     tyc = jnp.broadcast_to(jnp.asarray(np.cos(angle), f32)[:, :, None], (8, 128, 128))
@@ -625,9 +740,13 @@
     dma = pltpu.SemaphoreType.DMA
     return pl.pallas_call(
         spectral_kernel,
-        out_shape=jax.ShapeDtypeStruct((SLOTS, WIDE, 40, 128), i32),
-        in_specs=[vmem] * 13,
-        out_specs=pl.BlockSpec(memory_space=pl.ANY),
+        out_shape=(
+            jax.ShapeDtypeStruct((SLOTS, WIDE, 40, 128), i32),
+            jax.ShapeDtypeStruct((WIDE, 64, 640), bf16),
+            jax.ShapeDtypeStruct((16, 8, 128), i32),
+        ),
+        in_specs=[vmem] * 17,
+        out_specs=(pl.BlockSpec(memory_space=pl.ANY), pl.BlockSpec(memory_space=pl.ANY), vmem),
         scratch_shapes=[
             pltpu.VMEM((2048, 128), f32),
             pltpu.VMEM((2048, 128), f32),
@@ -649,11 +768,19 @@
             pltpu.VMEM((8, 128, 128), i32),
             pltpu.VMEM((8, 128, 128), i32),
             pltpu.VMEM((8, 8, 128), i32),
+            pltpu.VMEM((NARROW, ROOM, 512), bf16),
+            pltpu.VMEM((NARROW, ROOM, 512), bf16),
+            pltpu.VMEM((NARROW, 16, ROOM), bf16),
+            pltpu.VMEM((NARROW, 16, ROOM), bf16),
+            pltpu.VMEM((WIDE, 64, 640), bf16),
+            pltpu.VMEM((WIDE, 64, 640), bf16),
             dma((SLOTS, WIDE)), dma((SLOTS, WIDE)),
             dma((SLOTS, NARROW)), dma((SLOTS, NARROW)),
             dma((SLOTS, NARROW)), dma((SLOTS, NARROW)),
             dma((SLOTS, WIDE)), dma((SLOTS, WIDE)),
             dma((2,)), dma((2,)),
+            dma((NARROW,)), dma((NARROW,)), dma((NARROW,)), dma((NARROW,)),
+            dma((WIDE,)), dma((WIDE,)), dma((1,)),
         ],
         compiler_params=pltpu.CompilerParams(
             collective_id=0, has_side_effects=True, vmem_limit_bytes=56 * 1024 * 1024
@@ -661,58 +788,58 @@
     )(
         noise.reshape(4096, 128), spectrum.reshape(4096, 128), t["tz"], t["yf"], t["yi"],
         t["xf"], t["xi"], tyc, tys, t["tx"], t["own2"], t["mir"], t["flips"],
+        place, parts, weights, JOIN,
     )
 
 
-def finish_kernel(
-    cell_row, target, freq, tzi, depth_at, assay, weight, out,
-    got, contrib, *accs,
-):
+def finish_kernel(numbers, freq, tzi, held, out, gathered, contrib, *accs):
     for acc in accs:
         acc[...] = jnp.zeros_like(acc)
 
-    def depth(y, _):
-        re, im = unpack(freq[pl.ds(y, 64, stride=40), :])
-        d = decode_factor(freq[pl.ds(32 + lax.rem(y, 8), 64, stride=40), :])
-        h, l = halves(jnp.concatenate([re * d, im * d], axis=0))
-        u = jnp.concatenate([h, h, l], axis=0)
-        out[pl.ds(y, 128, stride=32), :] = lax.dot_general(
-            u, tzi[...], (((0,), (0,)), ((), ())), preferred_element_type=f32
-        )
-        return 0
-
-    lax.fori_loop(0, 32, depth, 0)
-    count = got.shape[0]
+    def depth(g, _):
+        for j in range(4):
+            y = g * 4 + j
+            re, im = unpack(freq[pl.ds(y, 64, stride=40), :])
+            d = decode_factor(freq[pl.ds(32 + lax.rem(y, 8), 64, stride=40), :])
+            h, l = halves(jnp.concatenate([re * d, im * d], axis=0))
+            u = jnp.concatenate([h, h, l], axis=0)
+            out[pl.ds(y, 128, stride=32), :] = lax.dot_general(
+                u, tzi[...], (((0,), (0,)), ((), ())), preferred_element_type=f32
+            )
+        return 0
+
+    lax.fori_loop(0, 8, depth, 0)
+    groups = numbers.shape[0]
 
     def gather(g, _):
-        for k in range(16):
-            i = g * 16 + k
-            got[pl.ds(i, 1), :] = out[pl.ds(cell_row[i], 1), :]
-        return 0
-
-    lax.fori_loop(0, count // 16, gather, 0)
+        for j in range(128):
+            gathered[pl.ds(g * 128 + j, 1), :] = out[pl.ds(numbers[g, 0, j], 1), :]
+        return 0
+
+    lax.fori_loop(0, groups, gather, 0)
     lane = lax.broadcasted_iota(i32, (128, 128), 1)
 
     def residual(g, _):
         at = rows16(g * 128, 128)
-        value = jnp.sum(jnp.where(lane == depth_at[at, :], got[at, :], 0.0), axis=1, keepdims=True)
-        resid = assay[at, :] - value
+        depth_at = held[at, 515:516].astype(i32)
+        grade = held[at, 524:525].astype(f32)
+        value = jnp.sum(jnp.where(lane == depth_at, gathered[at, :], 0.0), axis=1, keepdims=True)
+        resid = grade - value
         for k in range(TARGETS):
-            contrib[k, at, :] = resid * weight[at, 128 * k : 128 * k + 128].astype(f32)
-        return 0
-
-    lax.fori_loop(0, count // 128, residual, 0)
+            contrib[k, at, :] = resid * held[at, 128 * k : 128 * k + 128].astype(f32)
+        return 0
+
+    lax.fori_loop(0, groups, residual, 0)
 
     def scatter(g, _):
-        for k in range(4):
-            i = g * 4 + k
+        for j in range(128):
             for t in range(TARGETS):
-                acc = accs[t + TARGETS * (k % 2)]
-                at = pl.ds(target[i * TARGETS + t], 1)
-                acc[at, :] = acc[at, :] + contrib[t, pl.ds(i, 1), :]
-        return 0
-
-    lax.fori_loop(0, count // 4, scatter, 0)
+                acc = accs[t + TARGETS * (j % 2)]
+                at = pl.ds(numbers[g, 1 + t, j], 1)
+                acc[at, :] = acc[at, :] + contrib[t, pl.ds(g * 128 + j, 1), :]
+        return 0
+
+    lax.fori_loop(0, groups, scatter, 0)
 
     def combine(g, _):
         at = rows(g * 64, 64)
@@ -725,63 +852,44 @@
     lax.fori_loop(0, 64, combine, 0)
 
 
-def finish(freq, cell, target, assay, weight):
+def finish(freq, held, numbers):
     vmem = pl.BlockSpec(memory_space=pltpu.VMEM)
     smem = pl.BlockSpec(memory_space=pltpu.SMEM)
-    count = cell.shape[0]
+    count = held.shape[0] * held.shape[1]
     return pl.pallas_call(
         finish_kernel,
         out_shape=jax.ShapeDtypeStruct((4096, 128), f32),
-        in_specs=[smem, smem] + [vmem] * 5,
+        in_specs=[smem] + [vmem] * 3,
         out_specs=vmem,
         scratch_shapes=[pltpu.VMEM((count, 128), f32), pltpu.VMEM((TARGETS, count, 128), f32)]
         + [pltpu.VMEM((4096, 128), f32)] * 8,
         compiler_params=pltpu.CompilerParams(vmem_limit_bytes=56 * 1024 * 1024),
-    )(
-        cell // NZ, target.reshape(-1), freq.reshape(-1, 128), TABLES["tzi"],
-        (cell % NZ)[:, None], assay[:, None], weight,
-    )
-
-
-def deliver(assay, weights, owner, cell, pencils):
+    )(numbers, freq.reshape(-1, 128), TABLES["tzi"], held.reshape(count, -1))
+
+
+def describe(assay, owner, cell, pencils):
     count = owner.shape[0]
-    capacity = max(4, 4 * count // (WIDE * NARROW))
     order = jnp.arange(count, dtype=i32)
-    earlier = (order[None, :] < order[:, None]) & (owner[None, :] == owner[:, None])
-    slot = owner * capacity + jnp.sum(earlier, axis=1, dtype=i32)
-    total = WIDE * NARROW * capacity
-    hot = jnp.arange(total, dtype=i32)[:, None] == slot[None, :]
-    placed = jnp.dot(hot.astype(bf16), weights, preferred_element_type=bf16)
-    fields = jnp.concatenate(
-        [cell[None], pencils.T, jnp.zeros((3, count), i32)], axis=0
-    ).astype(f32)
-    numbers = lax.dot_general(
-        fields, hot.astype(f32), (((1,), (1,)), ((), ())), precision=lax.Precision.HIGHEST
-    )
-    numbers = jnp.round(numbers).astype(i32)
-    grade = jnp.sum(jnp.where(hot, assay.astype(f32)[None, :], 0.0), axis=1).astype(bf16)
-
-    def both(x):
-        x = lax.all_to_all(x, "wide", split_axis=0, concat_axis=0, tiled=True)
-        return lax.all_to_all(x, "narrow", split_axis=1, concat_axis=1, tiled=True)
-
-    placed = both(placed.reshape(WIDE, NARROW, capacity, TARGETS * NZ)).reshape(total, TARGETS * NZ)
-    numbers = numbers.reshape(8, WIDE, NARROW, capacity).transpose(1, 2, 0, 3)
-    numbers = both(numbers.reshape(WIDE, NARROW, 8 * capacity))
-    numbers = numbers.reshape(WIDE * NARROW, 8, capacity).transpose(1, 0, 2).reshape(8, total)
-    grade = both(grade.reshape(WIDE, NARROW, capacity)).reshape(total)
-    return numbers[0], numbers[1 : 1 + TARGETS].T, grade.astype(f32), placed
+    earlier = order[:, None] < order[None, :]
+    narrow = owner % NARROW
+    rank = jnp.sum(earlier & (narrow[:, None] == narrow[None, :]), axis=0, dtype=i32)
+    same = jnp.sum(earlier & (owner[:, None] == owner[None, :]), axis=0, dtype=i32)
+    place = (narrow * ROOM + rank)[None]
+    key = owner // NARROW * 8 + same + 1
+    row = cell // NZ
+    fields = [key, row // 256, row % 256, cell % NZ]
+    for k in range(TARGETS):
+        fields += [pencils[:, k] // 256, pencils[:, k] % 256]
+    fields = [x.astype(bf16) for x in fields] + [assay] + [jnp.zeros((count,), bf16)] * 3
+    return place, jnp.stack(fields)
 
 
 def local(noise, spectrum, assay, measure_weights, measure_owner, measure_cell, measure_pencils):
     count = measure_owner.shape[1]
-    cell, target, grade, placed = deliver(
-        assay[0], measure_weights[0].reshape(count, TARGETS * NZ), measure_owner[0],
-        measure_cell[0], measure_pencils[0],
-    )
-    freq = spectral(noise, spectrum)
-    field = finish(freq, cell, target, grade, placed)
-    return field.reshape(noise.shape)
+    place, parts = describe(assay[0], measure_owner[0], measure_cell[0], measure_pencils[0])
+    weights = measure_weights[0].reshape(count, TARGETS * NZ)
+    freq, held, numbers = spectral(noise, spectrum, place, parts, weights)
+    return finish(freq, held, numbers).reshape(noise.shape)
 
 
 def solution(mesh):

time: 276 us -> 204 us (0.74)
  waiting for transfers between devices: 41.2 us -> 0 us
  starting transfers between devices: 35.7 us -> 0 us
  Pallas kernels: 166 us -> 190 us
  local copies, waits for them, and re-layouts: 19.8 us -> 7.25 us
  matrix products: 5.18 us -> 0 us
    all_to_all x6 -> x0, waiting for transfers between devices: 41.2 us -> none  [the longest x3 35.4 us: both(): x = lax.all_to_all(x, 'wide', split_axis=0, concat_axis=0, tiled=True)]
    all_to_all x6 -> x0, starting transfers between devices: 35.7 us -> none  [the longest x3 18.6 us: both(): return lax.all_to_all(x, 'narrow', split_axis=1, concat_axis=1, tiled=True)]
    pallas_call x1, Pallas kernels: 135 us -> 167 us  [spectral(): pl.pallas_call(spectral_kernel, out_shape=(jax.ShapeDtypeStruct((SLOTS, W...]
    pallas_call x1, Pallas kernels: 30.4 us -> 23.5 us  [finish(): pl.pallas_call(finish_kernel, out_shape=jax.ShapeDtypeStruct((4096, 128),...]
    dot_general x2 -> x0, matrix products: 5.18 us -> none  [the longest x1 2.67 us: deliver(): lax.dot_general(fields, hot.astype(f32), (((1,), (1,)), ((), ())), precis...]
    all_to_all x6 -> x0, local copies, waits for them, and re-layouts: 4.7 us -> none  [the longest x2 2.55 us: both(): return lax.all_to_all(x, 'narrow', split_axis=1, concat_axis=1, tiled=True)]
    convert_element_type x0 -> x6, other arithmetic: none -> 3.91 us  [describe(): x.astype(bf16)]
    reshape x4 -> x0, local copies, waits for them, and re-layouts: 3.69 us -> none  [the longest x1 2.44 us: finish(): target.reshape(-1)]
  transfers between devices with their start and end apart: 6 -> 0, of which waited for: 5 -> 0; matrix products, arithmetic and copies ran while one was open for 9% -> 0% of each run, Pallas kernels for 49% -> 0%
where the time goes in v2:
time: 204 us
  Pallas kernels  190 us (93%)
  local copies, waits for them, and re-layouts  7.25 us (4%)
  other arithmetic  6.31 us (3%)
    pallas_call x1, Pallas kernels, spectral(): pl.pallas_call(spectral_kernel, out_shape=(jax.ShapeDtypeStruct((SLOTS, W...  167 us
    pallas_call x1, Pallas kernels, finish(): pl.pallas_call(finish_kernel, out_shape=jax.ShapeDtypeStruct((4096, 128),...  23.5 us

profile of v2, /device:TPU:65, one launch (start us, length us, event | category | flops | bytes accessed | tf_op | source)
XLA Modules:
  0.0 203.8 jit_solution(4184127965384417893)
XLA Ops:
  0.0 0.9 convert_reduce_fusion
  0.9 0.7 add_select_fusion
  1.6 0.7 add_convert_fusion
  2.3 0.2 convert_reduce_fusion.1
  2.5 0.6 multiply_add_fusion.place
  3.1 0.7 fusion.4
  3.8 0.8 fusion.8
  4.6 0.8 fusion.3
  5.5 0.8 fusion.12
  6.3 1.9 stack.5.parts
  8.3 1.9 copy.23
  10.2 1.7 broadcast_in_dim.4.tyc
  11.9 1.7 broadcast_in_dim.5.tys
  13.6 166.7 %shard_map.190 = (s32[2,32,40,128]{3,2,1,0:T(8,128)}, bf16[32,64,640]{2,1,0:T(8,128)(2,1)}, s32[16,8,128]{2,1,0:T(8,128)}) custom-call(f32[4096,128]{1,0:T(8,128)} %bitcast.44, f32[4096,128]{1,0:T(8,128)} %bitcast.45, bf16[128,384]{1,0:T(8,128)(2,1)} %constant.147.clone.tz, bf16[2,256,256]{2,1,0:T(8,128)(2,1)} %constant.148.clone.yf.xi, ...), custom_call_target="tpu_custom_call" | custom-call | tf_op jit(solution)/shard_map/pallas_call | solution.py:741
  180.3 23.5 %shard_map.191 = f32[4096,128]{1,0:T(8,128)} custom-call(s32[16,8,128]{2,1,0:T(8,128)} %get-tuple-element.8.numbers, s32[2560,128]{1,0:T(8,128)} %bitcast.47, bf16[384,128]{1,0:T(8,128)(2,1)} %constant.155.clone.tzi, bf16[2048,640]{1,0:T(8,128)(2,1)} %bitcast.43), custom_call_target="tpu_custom_call" | custom-call | tf_op jit(solution)/shard_map/pallas_call | solution.py:859
  (3 shorter events, 0.0 us)

commit v3 on v2

--- a/solution.py
+++ b/solution.py
@@ -89,7 +89,7 @@
 
 
 TABLES = make_tables()
-ROOM = 256
+ROOM = 160
 
 
 def join_matrix():
@@ -97,6 +97,7 @@
     m[0, 1], m[0, 2] = 256, 1
     for k in range(TARGETS):
         m[1 + k, 4 + 2 * k], m[1 + k, 5 + 2 * k] = 256, 1
+    m[5, 13] = 1
     return m.astype(ml_dtypes.bfloat16)
 
 
@@ -194,10 +195,10 @@
 
 
 def spectral_kernel(
-    noise, spec, tz, yf, yi, xf, xi, tyc, tys, tx, own2, mir, flips, place, parts, weights, join,
-    out, got, numbers,
+    noise, spec, tz, yf, yi, xf, xi, tyc, tys, tx, own2, mir, flips, owner, cell, assay, pencils, loads, join,
+    out, got, numbers, flag,
     zre, zim, ws, wr, bh, bl, big, big2, ns, nr, lh, ll, ms, mr, us,
-    ear, bsp, vs, vr, vc, asend, arecv, psend, precv, bsend, brecv,
+    ear, bsp, vs, vr, vc, wf, weights, parts, asend, arecv, psend, precv, bsend, brecv,
     w_send, w_recv, n_send, n_recv, m_send, m_recv, u_send, u_recv, v_send, v_recv,
     a_send, a_recv, p_send, p_recv, b_send, b_recv, g_sem,
 ):
@@ -301,13 +302,53 @@
         vc[...] = vs[:, 0:8, :]
 
     room = asend.shape[1]
-    count = place.shape[1]
+    count = owner.shape[1]
+    owners = owner[...]
+    cells = cell[...]
+    narrow_of = (owners & 7).astype(f32)
+    diagonal = lax.broadcasted_iota(i32, (128, 128), 0) == lax.broadcasted_iota(i32, (128, 128), 1)
+
+    def column(line):
+        pieces = []
+        for k in range(count // 128):
+            piece = jnp.broadcast_to(line[:, 128 * k : 128 * k + 128], (128, 128))
+            pieces.append(jnp.sum(jnp.where(diagonal, piece, 0.0), axis=1, keepdims=True))
+        return jnp.concatenate(pieces, axis=0)
+
+    earlier = lax.broadcasted_iota(i32, (count, count), 0) < lax.broadcasted_iota(i32, (count, count), 1)
+
+    def before(line):
+        match = earlier & (column(line) == line)
+        return jnp.sum(jnp.where(match, 1.0, 0.0), axis=0, keepdims=True)
+
+    same = before(owners.astype(f32))
+    rank = before(narrow_of)
+    place = jnp.where(rank < room, narrow_of * room + rank, -1.0).astype(i32)
+    over = jnp.max(jnp.where(rank < room, 0.0, 1.0), axis=1, keepdims=True)
+    key = (owners >> 3 << 3).astype(f32) + same + 1.0
+    part_row = lax.broadcasted_iota(i32, (16, count), 0)
+    listed = jnp.zeros((16, count), f32)
+    for r, line in (
+        (0, key),
+        (1, (cells >> 15).astype(f32)),
+        (2, ((cells >> 7) & 255).astype(f32)),
+        (3, (cells & 127).astype(f32)),
+        (12, assay[...].astype(f32)),
+        *((4 + 2 * k, (pencils[k : k + 1, :] >> 8).astype(f32)) for k in range(TARGETS)),
+        *((5 + 2 * k, (pencils[k : k + 1, :] & 255).astype(f32)) for k in range(TARGETS)),
+    ):
+        listed = jnp.where(part_row == r, line, listed)
+    parts[...] = listed.astype(bf16)
+    wf[...] = loads[...].astype(f32)
+    for k in range(TARGETS):
+        weights[:, 128 * k : 128 * k + 128] = wf[pl.ds(k, count, stride=TARGETS), :].astype(bf16)
     room_row = lax.broadcasted_iota(i32, (room, count), 0)
+    flag_row = lax.broadcasted_iota(i32, (16, room), 0) == 13
 
     def pack_measures(n, _):
-        hot = jnp.where(room_row + n * room == place[...], 1.0, 0.0).astype(bf16)
+        hot = jnp.where(room_row + n * room == place, 1.0, 0.0).astype(bf16)
         asend[n] = mm(hot, weights[...]).astype(bf16)
-        psend[n] = mm_t(parts[...], hot).astype(bf16)
+        psend[n] = jnp.where(flag_row, over, mm_t(parts[...], hot)).astype(bf16)
         return 0
 
     lax.fori_loop(0, NARROW, pack_measures, 0)
@@ -360,6 +401,14 @@
         peer = lax.rem(me_w + i, WIDE)
         to_wide(peer, peer).wait_send()
         return 0
+
+    pl.semaphore_wait(barrier, WIDE - 1 + NARROW - 1)
+    lax.fori_loop(1, NARROW, send_measures, 0)
+    v_main.start()
+
+    @pl.when(jnp.logical_not(alone))
+    def _():
+        v_side.start()
 
     def depth(y, _):
         cells = [y * 4 + k for k in range(4)]
@@ -396,17 +445,7 @@
 
         lax.fori_loop(0, WIDE, code_one, 0)
         wr[s, me_w] = ws[s, me_w]
-        if s == 0:
-            pl.semaphore_wait(barrier, WIDE - 1 + NARROW - 1)
         send_all(wide_copy, WIDE, me_w, w_args, s)
-        if s == 0:
-            v_main.start()
-
-            @pl.when(jnp.logical_not(alone))
-            def _():
-                v_side.start()
-
-            lax.fori_loop(1, NARROW, send_measures, 0)
 
     def second_forward(s, p, q, r):
         def group(g, _):
@@ -485,19 +524,23 @@
     lax.fori_loop(1, NARROW, recv_measures, 0)
     row = lax.broadcasted_iota(i32, (512, room), 0)
     want = (((row >> 4) << 3) + (row & 7) + 1).astype(f32)
+    flags = precv[0].astype(f32)
+    for k in range(1, NARROW):
+        flags = jnp.maximum(flags, precv[k].astype(f32))
+    flags = jnp.max(jnp.where(flag_row, flags, 0.0), axis=1, keepdims=True)
+    flags = jnp.max(flags, axis=0, keepdims=True)
+    flag_col = lax.broadcasted_iota(i32, (512, 128), 1) == 13
     for q in range(4):
-        hot = []
+        moved, named = 0.0, 0.0
         for k in range(2):
             key = precv[2 * q + k, 0:1, :].astype(f32)
             match = (((row >> 3) & 1) == k) & (want == key)
-            hot.append(jnp.where(match, 1.0, 0.0).astype(bf16))
-        hot = jnp.concatenate(hot, axis=1)
-        held = jnp.concatenate([arecv[2 * q], arecv[2 * q + 1]], axis=0)
-        names = jnp.concatenate([precv[2 * q], precv[2 * q + 1]], axis=1)
-        moved = mm(hot, held).astype(bf16).reshape(WIDE, 16, 512)
-        named = mm_t(hot, names)
+            hot = jnp.where(match, 1.0, 0.0).astype(bf16)
+            moved = moved + mm(hot, arecv[2 * q + k])
+            named = named + mm_t(hot, precv[2 * q + k])
         named = jnp.concatenate([named, jnp.zeros((512, 112), f32)], axis=1)
-        bsend[:, 16 * q : 16 * q + 16, 0:512] = moved
+        named = jnp.where(flag_col, flags, named)
+        bsend[:, 16 * q : 16 * q + 16, 0:512] = moved.astype(bf16).reshape(WIDE, 16, 512)
         bsend[:, 16 * q : 16 * q + 16, 512:640] = named.astype(bf16).reshape(WIDE, 16, 128)
     brecv[me_w] = bsend[me_w]
     lax.fori_loop(1, WIDE, send_groups, 0)
@@ -712,7 +755,10 @@
         named = jnp.concatenate(
             [brecv[2 * g, :, 512:640], brecv[2 * g + 1, :, 512:640]], axis=0
         )
-        numbers[g] = jnp.round(mm_t(join[...], named)).astype(i32)
+        listed = jnp.round(mm_t(join[...], named))
+        numbers[g] = listed.astype(i32)
+        marks = listed if g == 0 else jnp.maximum(marks, listed)
+    flag[...] = jnp.broadcast_to(jnp.max(marks, axis=1, keepdims=True), (8, 128)).astype(i32)
     lax.fori_loop(1, WIDE, sent_groups, 0)
     lax.fori_loop(1, NARROW, sent_measures, 0)
     pltpu.make_async_copy(brecv, got, g_sem.at[0]).wait()
@@ -731,11 +777,11 @@
         v_side.wait_send()
 
 
-def spectral(noise, spectrum, place, parts, weights):
+def spectral(noise, spectrum, owner, cell, assay, pencils, loads):
     t = TABLES
     angle = 2 * np.pi * np.arange(8)[:, None] * np.arange(128)[None, :] / 1024
-    tyc = jnp.broadcast_to(jnp.asarray(np.cos(angle), f32)[:, :, None], (8, 128, 128))
-    tys = jnp.broadcast_to(jnp.asarray(np.sin(angle), f32)[:, :, None], (8, 128, 128))
+    tyc = np.repeat(np.cos(angle).astype(np.float32)[:, :, None], 128, axis=2)
+    tys = np.repeat(np.sin(angle).astype(np.float32)[:, :, None], 128, axis=2)
     vmem = pl.BlockSpec(memory_space=pltpu.VMEM)
     dma = pltpu.SemaphoreType.DMA
     return pl.pallas_call(
@@ -744,9 +790,10 @@
             jax.ShapeDtypeStruct((SLOTS, WIDE, 40, 128), i32),
             jax.ShapeDtypeStruct((WIDE, 64, 640), bf16),
             jax.ShapeDtypeStruct((16, 8, 128), i32),
+            jax.ShapeDtypeStruct((8, 128), i32),
         ),
-        in_specs=[vmem] * 17,
-        out_specs=(pl.BlockSpec(memory_space=pl.ANY), pl.BlockSpec(memory_space=pl.ANY), vmem),
+        in_specs=[vmem] * 19,
+        out_specs=(pl.BlockSpec(memory_space=pl.ANY), pl.BlockSpec(memory_space=pl.ANY), vmem, vmem),
         scratch_shapes=[
             pltpu.VMEM((2048, 128), f32),
             pltpu.VMEM((2048, 128), f32),
@@ -768,6 +815,9 @@
             pltpu.VMEM((8, 128, 128), i32),
             pltpu.VMEM((8, 128, 128), i32),
             pltpu.VMEM((8, 8, 128), i32),
+            pltpu.VMEM((2048, 128), f32),
+            pltpu.VMEM((512, 512), bf16),
+            pltpu.VMEM((16, 512), bf16),
             pltpu.VMEM((NARROW, ROOM, 512), bf16),
             pltpu.VMEM((NARROW, ROOM, 512), bf16),
             pltpu.VMEM((NARROW, 16, ROOM), bf16),
@@ -788,7 +838,7 @@
     )(
         noise.reshape(4096, 128), spectrum.reshape(4096, 128), t["tz"], t["yf"], t["yi"],
         t["xf"], t["xi"], tyc, tys, t["tx"], t["own2"], t["mir"], t["flips"],
-        place, parts, weights, JOIN,
+        owner, cell, assay, pencils, loads, JOIN,
     )
 
 
@@ -867,29 +917,45 @@
     )(numbers, freq.reshape(-1, 128), TABLES["tzi"], held.reshape(count, -1))
 
 
-def describe(assay, owner, cell, pencils):
+def padded(assay, weights, owner, cell, pencils):
     count = owner.shape[0]
     order = jnp.arange(count, dtype=i32)
     earlier = order[:, None] < order[None, :]
-    narrow = owner % NARROW
-    rank = jnp.sum(earlier & (narrow[:, None] == narrow[None, :]), axis=0, dtype=i32)
     same = jnp.sum(earlier & (owner[:, None] == owner[None, :]), axis=0, dtype=i32)
-    place = (narrow * ROOM + rank)[None]
-    key = owner // NARROW * 8 + same + 1
     row = cell // NZ
-    fields = [key, row // 256, row % 256, cell % NZ]
+    fields = [jnp.zeros((count,), i32), row // 256, row % 256, cell % NZ]
     for k in range(TARGETS):
         fields += [pencils[:, k] // 256, pencils[:, k] % 256]
-    fields = [x.astype(bf16) for x in fields] + [assay] + [jnp.zeros((count,), bf16)] * 3
-    return place, jnp.stack(fields)
+    fields = [x.astype(bf16) for x in fields] + [assay]
+    parts = jnp.zeros((count, 128), bf16).at[:, : len(fields)].set(jnp.stack(fields, axis=1))
+    load = jnp.concatenate([weights, parts], axis=1)
+    slots = jnp.arange(WIDE * NARROW * 8, dtype=i32)
+    hot = (slots[:, None] == (owner * 8 + same)[None, :]).astype(bf16)
+    held = jnp.dot(hot, load, preferred_element_type=f32).astype(bf16)
+    held = held.reshape(WIDE, NARROW, 8, -1)
+    held = lax.all_to_all(held, "wide", split_axis=0, concat_axis=0, tiled=True)
+    held = lax.all_to_all(held, "narrow", split_axis=1, concat_axis=1, tiled=True)
+    held = held.reshape(WIDE, 64, -1)
+    names = held.reshape(WIDE * 64, -1)[:, TARGETS * NZ :].astype(f32)
+    numbers = jnp.einsum("fc,gjc->gfj", jnp.asarray(JOIN, f32), names.reshape(16, 128, 128),
+                         precision=lax.Precision.HIGHEST)
+    return held, jnp.round(numbers).astype(i32)
 
 
 def local(noise, spectrum, assay, measure_weights, measure_owner, measure_cell, measure_pencils):
     count = measure_owner.shape[1]
-    place, parts = describe(assay[0], measure_owner[0], measure_cell[0], measure_pencils[0])
-    weights = measure_weights[0].reshape(count, TARGETS * NZ)
-    freq, held, numbers = spectral(noise, spectrum, place, parts, weights)
-    return finish(freq, held, numbers).reshape(noise.shape)
+    freq, held, numbers, flag = spectral(
+        noise, spectrum, measure_owner, measure_cell, assay, measure_pencils[0].T,
+        measure_weights.reshape(count * TARGETS, NZ),
+    )
+
+    def roomy(_):
+        weights = measure_weights[0].reshape(count, TARGETS * NZ)
+        more = padded(assay[0], weights, measure_owner[0], measure_cell[0], measure_pencils[0])
+        return finish(freq, *more)
+
+    field = lax.cond(flag[5, 0] > 0, roomy, lambda _: finish(freq, held, numbers), 0)
+    return field.reshape(noise.shape)
 
 
 def solution(mesh):

time: 204 us -> 161 us (0.79)
  Pallas kernels: 190 us -> 157 us
  other arithmetic: 6.31 us -> 0 us
  local copies, waits for them, and re-layouts: 7.25 us -> 2.52 us
    pallas_call x1, Pallas kernels: 167 us -> 135 us  [spectral(): pl.pallas_call(spectral_kernel, out_shape=(jax.ShapeDtypeStruct((SLOTS, W...]
    convert_element_type x6 -> x0, other arithmetic: 3.91 us -> none  [describe(): x.astype(bf16)]
    broadcast_in_dim x2 -> x0, local copies, waits for them, and re-layouts: 3.38 us -> none  [the longest x1 1.7 us: spectral(): jnp.broadcast_to(jnp.asarray(np.sin(angle), f32)[:, :, None], (8, 128, 128))]
where the time goes in v3:
time: 161 us; the launch traced here: 160 us
  Pallas kernels  157 us (98%)
  local copies, waits for them, and re-layouts  2.52 us (2%)
    pallas_call x1, Pallas kernels, spectral(): pl.pallas_call(spectral_kernel, out_shape=(jax.ShapeDtypeStruct((SLOTS, W...  135 us
    pallas_call x1, Pallas kernels, finish(): pl.pallas_call(finish_kernel, out_shape=jax.ShapeDtypeStruct((4096, 128),...  21.6 us

profile of v3, /device:TPU:65, one launch (start us, length us, event | category | flops | bytes accessed | tf_op | source)
XLA Modules:
  0.0 159.8 jit_solution(17905335871379266356)
XLA Ops:
  0.0 0.0 copy-start.2
  0.0 0.0 copy-start.3
  0.0 0.0 copy-start.4
  0.0 0.0 copy-start.5
  0.0 0.0 copy-start.6
  0.0 134.9 %shard_map.202 = (s32[2,32,40,128]{3,2,1,0:T(8,128)S(1)}, bf16[32,64,640]{2,1,0:T(8,128)(2,1)S(1)}, s32[16,8,128]{2,1,0:T(8,128)S(1)}, s32[8,128]{1,0:T(8,128)}) custom-call(f32[4096,128]{1,0:T(8,128)} %bitcast.52, f32[4096,128]{1,0:T(8,128)} %bitcast.53, bf16[128,384]{1,0:T(8,128)(2,1)} %constant.156.clone.tz, bf16[2,256,256]{2,1,0:T(8,128)(2,1)} %constant.157.clone.yf.xi, ...), custom_call_target="tpu_custom_call" | custom-call | tf_op jit(solution)/shard_map/pallas_call | solution.py:787
  135.0 1.2 slice.38
  136.8 0.0 copy-done.2
  136.8 0.0 copy-done.3
  136.8 0.0 copy-done.4
  136.8 0.0 copy-done.5
  136.8 0.0 copy-done.6
  136.9 21.6 %conditional.1 = (f32[128,32,128]{2,1,0:T(8,128)S(1)}) conditional(s32[]{:T(128)} %bitcast.21, (s32[2,32,40,128]{3,2,1,0:T(8,128)S(1)}, bf16[32,64,640]{2,1,0:T(8,128)(2,1)S(1)}, s32[16,8,128]{2,1,0:T(8,128)S(1)}, bf16[384,128]{1,0:T(8,128)(2,1)S(1)}) %tuple.45, (s32[1,512]{1,0:T(1,128)S(1)}, bf16[1,512,4,128]{3,2,1,0:T(4,128)(2,1)}, ...), branch_computations={%region_0.0_spmd, %region_1.4_spmd} | conditional | flops 1373095424 | bytes 37477444 | solution.py:957
  136.9 21.6 %branch_0_fun.1 = f32[4096,128]{1,0:T(8,128)S(1)} custom-call(s32[16,8,128]{2,1,0:T(8,128)S(1)} %get-tuple-element.45.numbers, s32[2560,128]{1,0:T(8,128)S(1)} %bitcast.45, bf16[384,128]{1,0:T(8,128)(2,1)S(1)} %get-tuple-element.47.tzi, bf16[2048,640]{1,0:T(8,128)(2,1)S(1)} %bitcast.47), custom_call_target="tpu_custom_call" | custom-call | tf_op jit(solution)/shard_map/cond/branch_0_fun/pallas_call | solution.py:909
  158.5 0.0 copy-start.1
  158.5 1.3 copy-done.1
Async XLA Ops:
  0.0 136.8 %copy-start.2 = (bf16[384,128]{1,0:T(8,128)(2,1)S(1)}, bf16[384,128]{1,0:T(8,128)(2,1)}, u32[]{:S(2)}) copy-start(bf16[384,128]{1,0:T(8,128)(2,1)} %constant.167.clone) | copy-start | bytes 294916
  0.0 136.8 %copy-start.3 = (s32[1,512,4]{1,2,0:T(4,128)S(1)}, s32[1,512,4]{1,2,0:T(4,128)}, u32[]{:S(2)}) copy-start(s32[1,512,4]{1,2,0:T(4,128)} %param.31) | copy-start | bytes 24580
  0.0 136.8 %copy-start.4 = (s32[1,512]{1,0:T(1,128)S(1)}, s32[1,512]{1,0:T(1,128)}, u32[]{:S(2)}) copy-start(s32[1,512]{1,0:T(1,128)} %owner.1) | copy-start | bytes 6148
  0.0 136.8 %copy-start.5 = (s32[1,512]{1,0:T(1,128)S(1)}, s32[1,512]{1,0:T(1,128)}, u32[]{:S(2)}) copy-start(s32[1,512]{1,0:T(1,128)} %cell.1) | copy-start | bytes 6148
  0.0 136.8 %copy-start.6 = (bf16[1,512]{1,0:T(2,128)(2,1)S(1)}, bf16[1,512]{1,0:T(2,128)(2,1)}, u32[]{:S(2)}) copy-start(bf16[1,512]{1,0:T(2,128)(2,1)} %assay.1) | copy-start | bytes 3076
  158.5 1.3 copy-start.1

commit v4 on v3

--- a/solution.py
+++ b/solution.py
@@ -62,7 +62,8 @@
     h, l = split(depth_forward())
     tz = np.concatenate([h, l, h], 1)
     h, l = split(depth_inverse())
-    tzi = np.concatenate([h, l, h], 0)
+    pick = [np.r_[32 * s : 32 * s + 32, 64 + 32 * s : 96 + 32 * s] for s in range(SLOTS)]
+    tzi = np.stack([np.concatenate([h[r], l[r], h[r]], 0) for r in pick])
     yf = np.stack(split(pair_matrix(-1.0)))
     yi = np.stack(split(pair_matrix(1.0)))
     xf = np.stack(split(pair_matrix(-1.0).T))
@@ -195,9 +196,9 @@
 
 
 def spectral_kernel(
-    noise, spec, tz, yf, yi, xf, xi, tyc, tys, tx, own2, mir, flips, owner, cell, assay, pencils, loads, join,
-    out, got, numbers, flag,
-    zre, zim, ws, wr, bh, bl, big, big2, ns, nr, lh, ll, ms, mr, us,
+    noise, spec, tz, yf, yi, xf, xi, tyc, tys, tx, own2, mir, flips, owner, cell, assay, pencils, loads, join, tzi,
+    field, got, numbers, flag,
+    zre, zim, ws, wr, bh, bl, big, big2, ns, nr, lh, ll, ms, mr, us, ur,
     ear, bsp, vs, vr, vc, wf, weights, parts, asend, arecv, psend, precv, bsend, brecv,
     w_send, w_recv, n_send, n_recv, m_send, m_recv, u_send, u_recv, v_send, v_recv,
     a_send, a_recv, p_send, p_recv, b_send, b_recv, g_sem,
@@ -262,7 +263,15 @@
     w_args = (ws, wr, w_send, w_recv)
     n_args = (ns, nr, n_send, n_recv)
     m_args = (ms, mr, m_send, m_recv)
-    u_args = (us, out, u_send, u_recv)
+    def back_rows(s, slot):
+        return ur.at[rows((s * WIDE + slot) * 40, 40), :]
+
+    def back_copy(s, peer, slot):
+        return pltpu.make_async_remote_copy(
+            src_ref=us.at[s, peer], dst_ref=back_rows(s, slot), send_sem=u_send.at[s, peer],
+            recv_sem=u_recv.at[s, slot], device_id={"wide": peer}, device_id_type=MESH,
+        )
+
 
     late = special & (me_n >= 4)
     own_slots = (jnp.where(late, 2, 0), 1)
@@ -300,6 +309,50 @@
     @pl.when(alone)
     def _():
         vc[...] = vs[:, 0:8, :]
+
+    pl.semaphore_wait(barrier, WIDE - 1 + NARROW - 1)
+    v_main.start()
+
+    @pl.when(jnp.logical_not(alone))
+    def _():
+        v_side.start()
+
+    def depth(y, _):
+        cells = [y * 4 + k for k in range(4)]
+        pieces = []
+        for k in cells:
+            h, l = halves(noise[pl.ds(k, 128, stride=32), :])
+            pieces.append(jnp.concatenate([h, h, l], axis=1))
+        res = mm_t(tz[...], jnp.concatenate(pieces, axis=0))
+        for i, k in enumerate(cells):
+            zre[pl.ds(k, 64, stride=32), :] = res[:64, 128 * i : 128 * i + 128]
+            zim[pl.ds(k, 64, stride=32), :] = res[64:, 128 * i : 128 * i + 128]
+        return 0
+
+    lax.fori_loop(0, 8, depth, 0)
+
+    def code_wide(read, dst, s, w, to):
+        re, im = read(w)
+        m = tile_max([re[8 * t : 8 * t + 8] for t in range(4)] + [im[8 * t : 8 * t + 8] for t in range(4)])
+        code = scale_code(m)
+        fac = encode_factor(code)
+        for t in range(4):
+            sl = slice(8 * t, 8 * t + 8)
+            dst[s, to, 8 * t : 8 * t + 8, :] = pack(re[sl] * fac, im[sl] * fac)
+        dst[s, to, 32:40, :] = code
+
+    for s in range(SLOTS):
+        def read_depth(w, s=s):
+            at = rows((s * 32 + w) * 32, 32)
+            return zre[at, :], zim[at, :]
+
+        def code_one(w, _, s=s, read=read_depth):
+            code_wide(read, ws, s, w, w)
+            return 0
+
+        lax.fori_loop(0, WIDE, code_one, 0)
+        wr[s, me_w] = ws[s, me_w]
+        send_all(wide_copy, WIDE, me_w, w_args, s)
 
     room = asend.shape[1]
     count = owner.shape[1]
@@ -402,50 +455,7 @@
         to_wide(peer, peer).wait_send()
         return 0
 
-    pl.semaphore_wait(barrier, WIDE - 1 + NARROW - 1)
     lax.fori_loop(1, NARROW, send_measures, 0)
-    v_main.start()
-
-    @pl.when(jnp.logical_not(alone))
-    def _():
-        v_side.start()
-
-    def depth(y, _):
-        cells = [y * 4 + k for k in range(4)]
-        pieces = []
-        for k in cells:
-            h, l = halves(noise[pl.ds(k, 128, stride=32), :])
-            pieces.append(jnp.concatenate([h, h, l], axis=1))
-        res = mm_t(tz[...], jnp.concatenate(pieces, axis=0))
-        for i, k in enumerate(cells):
-            zre[pl.ds(k, 64, stride=32), :] = res[:64, 128 * i : 128 * i + 128]
-            zim[pl.ds(k, 64, stride=32), :] = res[64:, 128 * i : 128 * i + 128]
-        return 0
-
-    lax.fori_loop(0, 8, depth, 0)
-
-    def code_wide(read, dst, s, w, to):
-        re, im = read(w)
-        m = tile_max([re[8 * t : 8 * t + 8] for t in range(4)] + [im[8 * t : 8 * t + 8] for t in range(4)])
-        code = scale_code(m)
-        fac = encode_factor(code)
-        for t in range(4):
-            sl = slice(8 * t, 8 * t + 8)
-            dst[s, to, 8 * t : 8 * t + 8, :] = pack(re[sl] * fac, im[sl] * fac)
-        dst[s, to, 32:40, :] = code
-
-    for s in range(SLOTS):
-        def read_depth(w, s=s):
-            at = rows((s * 32 + w) * 32, 32)
-            return zre[at, :], zim[at, :]
-
-        def code_one(w, _, s=s, read=read_depth):
-            code_wide(read, ws, s, w, w)
-            return 0
-
-        lax.fori_loop(0, WIDE, code_one, 0)
-        wr[s, me_w] = ws[s, me_w]
-        send_all(wide_copy, WIDE, me_w, w_args, s)
 
     def second_forward(s, p, q, r):
         def group(g, _):
@@ -745,12 +755,31 @@
             return 0
 
         lax.fori_loop(0, WIDE, code_back, 0)
-        keep = pltpu.make_async_copy(us.at[s, me_w], out.at[s, me_w], u_recv.at[s, me_w])
-        keep.start()
-        send_all(wide_copy, WIDE, me_w, u_args, s)
+        back_rows(s, me_w)[...] = us[s, me_w]
+        send_all(back_copy, WIDE, me_w, (), s)
+
+    def depth_back(s):
+        base = s * WIDE * 40
+
+        def some(g, _):
+            for j in range(4):
+                y = g * 4 + j
+                re, im = unpack(ur[pl.ds(base + y, WIDE, stride=40), :])
+                d = decode_factor(ur[pl.ds(base + 32 + lax.rem(y, 8), WIDE, stride=40), :])
+                h, l = halves(jnp.concatenate([re * d, im * d], axis=0))
+                u = jnp.concatenate([h, h, l], axis=0)
+                part = lax.dot_general(
+                    u, tzi[s], (((0,), (0,)), ((), ())), preferred_element_type=f32
+                )
+                at = pl.ds(y, 128, stride=32)
+                field[at, :] = part if s == 0 else field[at, :] + part
+            return 0
+
+        lax.fori_loop(0, 8, some, 0)
 
     lax.fori_loop(1, WIDE, recv_groups, 0)
-    pltpu.make_async_copy(brecv, got, g_sem.at[0]).start()
+    held = pltpu.make_async_copy(brecv, got, g_sem.at[0])
+    held.start()
     for g in range(16):
         named = jnp.concatenate(
             [brecv[2 * g, :, 512:640], brecv[2 * g + 1, :, 512:640]], axis=0
@@ -758,18 +787,19 @@
         listed = jnp.round(mm_t(join[...], named))
         numbers[g] = listed.astype(i32)
         marks = listed if g == 0 else jnp.maximum(marks, listed)
-    flag[...] = jnp.broadcast_to(jnp.max(marks, axis=1, keepdims=True), (8, 128)).astype(i32)
+    flag[0, 0] = jnp.max(marks[5:6, :]).astype(i32)
+    recv_all(back_copy, WIDE, me_w, (), 0)
+    depth_back(0)
+    recv_all(back_copy, WIDE, me_w, (), 1)
+    depth_back(1)
+    held.wait()
     lax.fori_loop(1, WIDE, sent_groups, 0)
     lax.fori_loop(1, NARROW, sent_measures, 0)
-    pltpu.make_async_copy(brecv, got, g_sem.at[0]).wait()
-
     for s in range(SLOTS):
-        pltpu.make_async_copy(us.at[s, me_w], out.at[s, me_w], u_recv.at[s, me_w]).wait()
-        recv_all(wide_copy, WIDE, me_w, u_args, s)
         sent_all(wide_copy, WIDE, me_w, w_args, s)
         sent_all(narrow_copy, NARROW, me_n, n_args, s)
         sent_all(narrow_copy, NARROW, me_n, m_args, s)
-        sent_all(wide_copy, WIDE, me_w, u_args, s)
+        sent_all(back_copy, WIDE, me_w, (), s)
     v_main.wait_send()
 
     @pl.when(jnp.logical_not(alone))
@@ -787,13 +817,15 @@
     return pl.pallas_call(
         spectral_kernel,
         out_shape=(
-            jax.ShapeDtypeStruct((SLOTS, WIDE, 40, 128), i32),
+            jax.ShapeDtypeStruct((4096, 128), f32),
             jax.ShapeDtypeStruct((WIDE, 64, 640), bf16),
             jax.ShapeDtypeStruct((16, 8, 128), i32),
-            jax.ShapeDtypeStruct((8, 128), i32),
+            jax.ShapeDtypeStruct((1, 1), i32),
         ),
-        in_specs=[vmem] * 19,
-        out_specs=(pl.BlockSpec(memory_space=pl.ANY), pl.BlockSpec(memory_space=pl.ANY), vmem, vmem),
+        in_specs=[vmem] * 20,
+        out_specs=(
+            vmem, pl.BlockSpec(memory_space=pl.ANY), vmem, pl.BlockSpec(memory_space=pltpu.SMEM),
+        ),
         scratch_shapes=[
             pltpu.VMEM((2048, 128), f32),
             pltpu.VMEM((2048, 128), f32),
@@ -810,6 +842,7 @@
             pltpu.VMEM((SLOTS, NARROW, 136, 128), i32),
             pltpu.VMEM((SLOTS, NARROW, 136, 128), i32),
             pltpu.VMEM((SLOTS, WIDE, 40, 128), i32),
+            pltpu.VMEM((SLOTS * WIDE * 40, 128), i32),
             pltpu.VMEM((SLOTS, 8, 128, 128), f32),
             pltpu.VMEM((8, 16, 128), f32),
             pltpu.VMEM((8, 128, 128), i32),
@@ -838,32 +871,19 @@
     )(
         noise.reshape(4096, 128), spectrum.reshape(4096, 128), t["tz"], t["yf"], t["yi"],
         t["xf"], t["xi"], tyc, tys, t["tx"], t["own2"], t["mir"], t["flips"],
-        owner, cell, assay, pencils, loads, JOIN,
+        owner, cell, assay, pencils, loads, JOIN, t["tzi"],
     )
 
 
-def finish_kernel(numbers, freq, tzi, held, out, gathered, contrib, *accs):
+def finish_kernel(numbers, field, held, out, gathered, contrib, sems, *accs):
     for acc in accs:
         acc[...] = jnp.zeros_like(acc)
 
-    def depth(g, _):
-        for j in range(4):
-            y = g * 4 + j
-            re, im = unpack(freq[pl.ds(y, 64, stride=40), :])
-            d = decode_factor(freq[pl.ds(32 + lax.rem(y, 8), 64, stride=40), :])
-            h, l = halves(jnp.concatenate([re * d, im * d], axis=0))
-            u = jnp.concatenate([h, h, l], axis=0)
-            out[pl.ds(y, 128, stride=32), :] = lax.dot_general(
-                u, tzi[...], (((0,), (0,)), ((), ())), preferred_element_type=f32
-            )
-        return 0
-
-    lax.fori_loop(0, 8, depth, 0)
     groups = numbers.shape[0]
 
     def gather(g, _):
         for j in range(128):
-            gathered[pl.ds(g * 128 + j, 1), :] = out[pl.ds(numbers[g, 0, j], 1), :]
+            gathered[pl.ds(g * 128 + j, 1), :] = field[pl.ds(numbers[g, 0, j], 1), :]
         return 0
 
     lax.fori_loop(0, groups, gather, 0)
@@ -891,30 +911,45 @@
 
     lax.fori_loop(0, groups, scatter, 0)
 
+    def leave(g):
+        at = rows(g * 256, 256)
+        return pltpu.make_async_copy(accs[0].at[at, :], out.at[at, :], sems.at[g])
+
     def combine(g, _):
-        at = rows(g * 64, 64)
-        v = out[at, :]
-        for acc in accs:
-            v = v + acc[at, :]
-        out[at, :] = v
-        return 0
-
-    lax.fori_loop(0, 64, combine, 0)
-
-
-def finish(freq, held, numbers):
+        for j in range(4):
+            at = rows(g * 256 + 64 * j, 64)
+            v = field[at, :]
+            for acc in accs:
+                v = v + acc[at, :]
+            accs[0][at, :] = v
+        leave(g).start()
+        return 0
+
+    def left(g, _):
+        leave(g).wait()
+        return 0
+
+    lax.fori_loop(0, 16, combine, 0)
+    lax.fori_loop(0, 16, left, 0)
+
+
+def finish(field, held, numbers):
     vmem = pl.BlockSpec(memory_space=pltpu.VMEM)
     smem = pl.BlockSpec(memory_space=pltpu.SMEM)
     count = held.shape[0] * held.shape[1]
     return pl.pallas_call(
         finish_kernel,
         out_shape=jax.ShapeDtypeStruct((4096, 128), f32),
-        in_specs=[smem] + [vmem] * 3,
-        out_specs=vmem,
-        scratch_shapes=[pltpu.VMEM((count, 128), f32), pltpu.VMEM((TARGETS, count, 128), f32)]
+        in_specs=[smem, vmem, vmem],
+        out_specs=pl.BlockSpec(memory_space=pltpu.HBM),
+        scratch_shapes=[
+            pltpu.VMEM((count, 128), f32),
+            pltpu.VMEM((TARGETS, count, 128), f32),
+            pltpu.SemaphoreType.DMA((16,)),
+        ]
         + [pltpu.VMEM((4096, 128), f32)] * 8,
         compiler_params=pltpu.CompilerParams(vmem_limit_bytes=56 * 1024 * 1024),
-    )(numbers, freq.reshape(-1, 128), TABLES["tzi"], held.reshape(count, -1))
+    )(numbers, field, held.reshape(count, -1))
 
 
 def padded(assay, weights, owner, cell, pencils):
@@ -944,7 +979,7 @@
 
 def local(noise, spectrum, assay, measure_weights, measure_owner, measure_cell, measure_pencils):
     count = measure_owner.shape[1]
-    freq, held, numbers, flag = spectral(
+    field, held, numbers, flag = spectral(
         noise, spectrum, measure_owner, measure_cell, assay, measure_pencils[0].T,
         measure_weights.reshape(count * TARGETS, NZ),
     )
@@ -952,10 +987,10 @@
     def roomy(_):
         weights = measure_weights[0].reshape(count, TARGETS * NZ)
         more = padded(assay[0], weights, measure_owner[0], measure_cell[0], measure_pencils[0])
-        return finish(freq, *more)
-
-    field = lax.cond(flag[5, 0] > 0, roomy, lambda _: finish(freq, held, numbers), 0)
-    return field.reshape(noise.shape)
+        return finish(field, *more)
+
+    done = lax.cond(flag[0, 0] > 0, roomy, lambda _: finish(field, held, numbers), 0)
+    return done.reshape(noise.shape)
 
 
 def solution(mesh):

time: 161 us -> 170 us (1.056)
  Pallas kernels: 157 us -> 168 us
    pallas_call x1, Pallas kernels: 135 us -> 148 us  [spectral(): pl.pallas_call(spectral_kernel, out_shape=(jax.ShapeDtypeStruct((4096, 12...]
where the time goes in v4:
time: 170 us
  Pallas kernels  168 us (99%)
    pallas_call x1, Pallas kernels, spectral(): pl.pallas_call(spectral_kernel, out_shape=(jax.ShapeDtypeStruct((4096, 12...  148 us
    pallas_call x1, Pallas kernels, finish(): pl.pallas_call(finish_kernel, out_shape=jax.ShapeDtypeStruct((4096, 128),...  20.2 us

profile of v4, /device:TPU:65, one launch (start us, length us, event | category | flops | bytes accessed | tf_op | source)
XLA Modules:
  0.0 170.2 jit_solution(9826264453282641720)
XLA Ops:
  0.0 0.0 copy-start.2
  0.0 0.0 copy-start.3
  0.0 0.0 copy-start.4
  0.0 0.0 copy-start.5
  0.0 0.0 copy-start.6
  0.0 147.9 %shard_map.202 = (f32[4096,128]{1,0:T(8,128)S(1)}, bf16[32,64,640]{2,1,0:T(8,128)(2,1)S(1)}, s32[16,8,128]{2,1,0:T(8,128)S(1)}, s32[1,1]{1,0:T(1,128)}) custom-call(f32[4096,128]{1,0:T(8,128)} %bitcast.48, f32[4096,128]{1,0:T(8,128)} %bitcast.49, bf16[128,384]{1,0:T(8,128)(2,1)} %constant.156.clone.tz, bf16[2,256,256]{2,1,0:T(8,128)(2,1)} %constant.157.clone.yf.xi, ...), custom_call_target="tpu_custom_call" | custom-call | tf_op jit(solution)/shard_map/pallas_call | solution.py:817
  148.5 0.0 copy-done.2
  148.5 0.0 copy-done.3
  148.5 0.0 copy-done.4
  148.6 0.0 copy-done.5
  148.6 0.0 copy-done.6
  148.6 20.3 %conditional.1 = (f32[128,32,128]{2,1,0:T(8,128)S(1)}) conditional(s32[]{:T(128)} %bitcast.19, (bf16[32,64,640]{2,1,0:T(8,128)(2,1)S(1)}, s32[16,8,128]{2,1,0:T(8,128)S(1)}, f32[4096,128]{1,0:T(8,128)S(1)}) %tuple.17, (s32[1,512]{1,0:T(1,128)S(1)}, bf16[1,512,4,128]{3,2,1,0:T(4,128)(2,1)S(1)}, s32[1,512]{1,0:T(1,128)S(1)}, ...), branch_computations={%region_0.0_spmd, %region_1.4_spmd} | conditional | flops 1373095424 | bytes 37477444 | solution.py:992
  148.6 20.2 %branch_0_fun.1 = f32[4096,128]{1,0:T(8,128)S(1)} custom-call(s32[16,8,128]{2,1,0:T(8,128)S(1)} %get-tuple-element.41.numbers, f32[4096,128]{1,0:T(8,128)S(1)} %get-tuple-element.42.field, bf16[2048,640]{1,0:T(8,128)(2,1)S(1)} %bitcast.43), custom_call_target="tpu_custom_call" | custom-call | tf_op jit(solution)/shard_map/cond/branch_0_fun/pallas_call | solution.py:940
  168.8 0.0 copy-start.1
  168.9 1.3 copy-done.1
Async XLA Ops:
  0.0 148.5 %copy-start.2 = (bf16[1,512,4,128]{3,2,1,0:T(4,128)(2,1)S(1)}, bf16[1,512,4,128]{3,2,1,0:T(4,128)(2,1)}, u32[]{:S(2)}) copy-start(bf16[1,512,4,128]{3,2,1,0:T(4,128)(2,1)} %param.28) | copy-start | bytes 1572868
  0.0 148.5 %copy-start.3 = (s32[1,512,4]{1,2,0:T(4,128)S(1)}, s32[1,512,4]{1,2,0:T(4,128)}, u32[]{:S(2)}) copy-start(s32[1,512,4]{1,2,0:T(4,128)} %param.31) | copy-start | bytes 24580
  0.0 148.5 %copy-start.4 = (s32[1,512]{1,0:T(1,128)S(1)}, s32[1,512]{1,0:T(1,128)}, u32[]{:S(2)}) copy-start(s32[1,512]{1,0:T(1,128)} %owner.1) | copy-start | bytes 6148
  0.0 148.5 %copy-start.5 = (s32[1,512]{1,0:T(1,128)S(1)}, s32[1,512]{1,0:T(1,128)}, u32[]{:S(2)}) copy-start(s32[1,512]{1,0:T(1,128)} %cell.1) | copy-start | bytes 6148
  0.0 148.5 %copy-start.6 = (bf16[1,512]{1,0:T(2,128)(2,1)S(1)}, bf16[1,512]{1,0:T(2,128)(2,1)}, u32[]{:S(2)}) copy-start(bf16[1,512]{1,0:T(2,128)(2,1)} %assay.1) | copy-start | bytes 3076
  168.8 1.3 copy-start.1

commit v5 on v3

--- a/solution.py
+++ b/solution.py
@@ -264,43 +264,6 @@
     m_args = (ms, mr, m_send, m_recv)
     u_args = (us, out, u_send, u_recv)
 
-    late = special & (me_n >= 4)
-    own_slots = (jnp.where(late, 2, 0), 1)
-    mir_slots = (jnp.where(special & (me_n < 4), 2, jnp.where(special, 0, 2)), 3)
-
-    def spectrum_rows(slot, e):
-        return halves(spec[pl.ds(slot * 1024 + e, 128, stride=8), :])
-
-    for e in range(8):
-        back = (8 - e) % 8
-        flip = flips[0 if e == 0 else 1]
-        codes = []
-        for s in range(SLOTS):
-            h, l = spectrum_rows(own_slots[s], e)
-            ear[s, e] = mm_t(own2[...], jnp.concatenate([h, l], axis=1))
-            h, l = spectrum_rows(mir_slots[s], back)
-            gh = mm_t(mir[...], h).astype(bf16)
-            gl = mm_t(mir[...], l).astype(bf16)
-            v = mm(jnp.concatenate([gh, gl], axis=1), flip)
-            q = jnp.round((jnp.log(v) - SPEC_LOW) * SPEC_CODE - 32500.0)
-            codes.append(jnp.clip(q, -32767.0, 32767.0))
-        vs[e] = pack(codes[0], codes[1])
-
-    v_main = pltpu.make_async_remote_copy(
-        src_ref=vs, dst_ref=vr, send_sem=v_send.at[0], recv_sem=v_recv.at[0],
-        device_id={"narrow": 7 - me_n}, device_id_type=MESH,
-    )
-    v_side = pltpu.make_async_remote_copy(
-        src_ref=vs.at[:, pl.ds(0, 8), :], dst_ref=vc, send_sem=v_send.at[1], recv_sem=v_recv.at[1],
-        device_id={"narrow": lax.rem(8 - me_n, 8)}, device_id_type=MESH,
-    )
-
-    alone = (me_n == 0) | (me_n == 4)
-
-    @pl.when(alone)
-    def _():
-        vc[...] = vs[:, 0:8, :]
-
     room = asend.shape[1]
     count = owner.shape[1]
     owners = owner[...]
@@ -404,6 +367,44 @@
 
     pl.semaphore_wait(barrier, WIDE - 1 + NARROW - 1)
     lax.fori_loop(1, NARROW, send_measures, 0)
+
+    late = special & (me_n >= 4)
+    own_slots = (jnp.where(late, 2, 0), 1)
+    mir_slots = (jnp.where(special & (me_n < 4), 2, jnp.where(special, 0, 2)), 3)
+
+    def spectrum_rows(slot, e):
+        return halves(spec[pl.ds(slot * 1024 + e, 128, stride=8), :])
+
+    for e in range(8):
+        back = (8 - e) % 8
+        flip = flips[0 if e == 0 else 1]
+        codes = []
+        for s in range(SLOTS):
+            h, l = spectrum_rows(own_slots[s], e)
+            ear[s, e] = mm_t(own2[...], jnp.concatenate([h, l], axis=1))
+            h, l = spectrum_rows(mir_slots[s], back)
+            gh = mm_t(mir[...], h).astype(bf16)
+            gl = mm_t(mir[...], l).astype(bf16)
+            v = mm(jnp.concatenate([gh, gl], axis=1), flip)
+            q = jnp.round((jnp.log(v) - SPEC_LOW) * SPEC_CODE - 32500.0)
+            codes.append(jnp.clip(q, -32767.0, 32767.0))
+        vs[e] = pack(codes[0], codes[1])
+
+    v_main = pltpu.make_async_remote_copy(
+        src_ref=vs, dst_ref=vr, send_sem=v_send.at[0], recv_sem=v_recv.at[0],
+        device_id={"narrow": 7 - me_n}, device_id_type=MESH,
+    )
+    v_side = pltpu.make_async_remote_copy(
+        src_ref=vs.at[:, pl.ds(0, 8), :], dst_ref=vc, send_sem=v_send.at[1], recv_sem=v_recv.at[1],
+        device_id={"narrow": lax.rem(8 - me_n, 8)}, device_id_type=MESH,
+    )
+
+    alone = (me_n == 0) | (me_n == 4)
+
+    @pl.when(alone)
+    def _():
+        vc[...] = vs[:, 0:8, :]
+
     v_main.start()
 
     @pl.when(jnp.logical_not(alone))
@@ -518,6 +519,8 @@
 
         lax.fori_loop(0, NARROW, code_n, 0)
         nr[s, me_n] = ns[s, me_n]
+        if s == 1:
+            sent_all(narrow_copy, NARROW, me_n, n_args, 0)
         send_all(narrow_copy, NARROW, me_n, n_args, s)
 
 
@@ -758,7 +761,7 @@
         listed = jnp.round(mm_t(join[...], named))
         numbers[g] = listed.astype(i32)
         marks = listed if g == 0 else jnp.maximum(marks, listed)
-    flag[...] = jnp.broadcast_to(jnp.max(marks, axis=1, keepdims=True), (8, 128)).astype(i32)
+    flag[0, 0] = jnp.max(marks[5:6, :]).astype(i32)
     lax.fori_loop(1, WIDE, sent_groups, 0)
     lax.fori_loop(1, NARROW, sent_measures, 0)
     pltpu.make_async_copy(brecv, got, g_sem.at[0]).wait()
@@ -767,7 +770,8 @@
         pltpu.make_async_copy(us.at[s, me_w], out.at[s, me_w], u_recv.at[s, me_w]).wait()
         recv_all(wide_copy, WIDE, me_w, u_args, s)
         sent_all(wide_copy, WIDE, me_w, w_args, s)
-        sent_all(narrow_copy, NARROW, me_n, n_args, s)
+        if s == 1:
+            sent_all(narrow_copy, NARROW, me_n, n_args, s)
         sent_all(narrow_copy, NARROW, me_n, m_args, s)
         sent_all(wide_copy, WIDE, me_w, u_args, s)
     v_main.wait_send()
@@ -790,10 +794,13 @@
             jax.ShapeDtypeStruct((SLOTS, WIDE, 40, 128), i32),
             jax.ShapeDtypeStruct((WIDE, 64, 640), bf16),
             jax.ShapeDtypeStruct((16, 8, 128), i32),
-            jax.ShapeDtypeStruct((8, 128), i32),
+            jax.ShapeDtypeStruct((1, 1), i32),
         ),
         in_specs=[vmem] * 19,
-        out_specs=(pl.BlockSpec(memory_space=pl.ANY), pl.BlockSpec(memory_space=pl.ANY), vmem, vmem),
+        out_specs=(
+            pl.BlockSpec(memory_space=pl.ANY), pl.BlockSpec(memory_space=pl.ANY), vmem,
+            pl.BlockSpec(memory_space=pltpu.SMEM),
+        ),
         scratch_shapes=[
             pltpu.VMEM((2048, 128), f32),
             pltpu.VMEM((2048, 128), f32),
@@ -954,7 +961,7 @@
         more = padded(assay[0], weights, measure_owner[0], measure_cell[0], measure_pencils[0])
         return finish(freq, *more)
 
-    field = lax.cond(flag[5, 0] > 0, roomy, lambda _: finish(freq, held, numbers), 0)
+    field = lax.cond(flag[0, 0] > 0, roomy, lambda _: finish(freq, held, numbers), 0)
     return field.reshape(noise.shape)
 
 

time: 161 us -> 168 us (1.043)
  the two profiles are of different devices: /device:TPU:65 before, /device:TPU:1 now
where the time goes in v5:
time: 168 us
  Pallas kernels  166 us (99%)
    pallas_call x1, Pallas kernels, spectral(): pl.pallas_call(spectral_kernel, out_shape=(jax.ShapeDtypeStruct((SLOTS, W...  144 us
    pallas_call x1, Pallas kernels, finish(): pl.pallas_call(finish_kernel, out_shape=jax.ShapeDtypeStruct((4096, 128),...  21.7 us

profile of v5, /device:TPU:1, one launch (start us, length us, event | category | flops | bytes accessed | tf_op | source)
XLA Modules:
  0.0 167.9 jit_solution(15906531181807149671)
XLA Ops:
  0.0 0.0 copy-start.2
  0.0 0.0 copy-start.3
  0.0 0.0 copy-start.4
  0.0 0.0 copy-start.5
  0.0 0.0 copy-start.6
  0.0 144.2 %shard_map.202 = (s32[2,32,40,128]{3,2,1,0:T(8,128)S(1)}, bf16[32,64,640]{2,1,0:T(8,128)(2,1)S(1)}, s32[16,8,128]{2,1,0:T(8,128)S(1)}, s32[1,1]{1,0:T(1,128)}) custom-call(f32[4096,128]{1,0:T(8,128)} %bitcast.52, f32[4096,128]{1,0:T(8,128)} %bitcast.53, bf16[128,384]{1,0:T(8,128)(2,1)} %constant.156.clone.tz, bf16[2,256,256]{2,1,0:T(8,128)(2,1)} %constant.157.clone.yf.xi, ...), custom_call_target="tpu_custom_call" | custom-call | tf_op jit(solution)/shard_map/pallas_call | solution.py:791
  144.9 0.0 copy-done.2
  144.9 0.0 copy-done.3
  144.9 0.0 copy-done.4
  144.9 0.0 copy-done.5
  144.9 0.0 copy-done.6
  144.9 21.7 %conditional.1 = (f32[128,32,128]{2,1,0:T(8,128)S(1)}) conditional(s32[]{:T(128)} %bitcast.21, (s32[2,32,40,128]{3,2,1,0:T(8,128)S(1)}, bf16[32,64,640]{2,1,0:T(8,128)(2,1)S(1)}, s32[16,8,128]{2,1,0:T(8,128)S(1)}, bf16[384,128]{1,0:T(8,128)(2,1)S(1)}) %tuple.45, (s32[1,512]{1,0:T(1,128)S(1)}, bf16[1,512,4,128]{3,2,1,0:T(4,128)(2,1)}, ...), branch_computations={%region_0.0_spmd, %region_1.4_spmd} | conditional | flops 1373095424 | bytes 37477444 | solution.py:964
  144.9 21.7 %branch_0_fun.1 = f32[4096,128]{1,0:T(8,128)S(1)} custom-call(s32[16,8,128]{2,1,0:T(8,128)S(1)} %get-tuple-element.45.numbers, s32[2560,128]{1,0:T(8,128)S(1)} %bitcast.45, bf16[384,128]{1,0:T(8,128)(2,1)S(1)} %get-tuple-element.47.tzi, bf16[2048,640]{1,0:T(8,128)(2,1)S(1)} %bitcast.47), custom_call_target="tpu_custom_call" | custom-call | tf_op jit(solution)/shard_map/cond/branch_0_fun/pallas_call | solution.py:916
  166.6 0.0 copy-start.1
  166.6 1.3 copy-done.1
Async XLA Ops:
  0.0 144.9 %copy-start.2 = (bf16[384,128]{1,0:T(8,128)(2,1)S(1)}, bf16[384,128]{1,0:T(8,128)(2,1)}, u32[]{:S(2)}) copy-start(bf16[384,128]{1,0:T(8,128)(2,1)} %constant.167.clone) | copy-start | bytes 294916
  0.0 144.9 %copy-start.3 = (s32[1,512,4]{1,2,0:T(4,128)S(1)}, s32[1,512,4]{1,2,0:T(4,128)}, u32[]{:S(2)}) copy-start(s32[1,512,4]{1,2,0:T(4,128)} %param.31) | copy-start | bytes 24580
  0.0 144.9 %copy-start.4 = (s32[1,512]{1,0:T(1,128)S(1)}, s32[1,512]{1,0:T(1,128)}, u32[]{:S(2)}) copy-start(s32[1,512]{1,0:T(1,128)} %owner.1) | copy-start | bytes 6148
  0.0 144.9 %copy-start.5 = (s32[1,512]{1,0:T(1,128)S(1)}, s32[1,512]{1,0:T(1,128)}, u32[]{:S(2)}) copy-start(s32[1,512]{1,0:T(1,128)} %cell.1) | copy-start | bytes 6148
  0.0 144.9 %copy-start.6 = (bf16[1,512]{1,0:T(2,128)(2,1)S(1)}, bf16[1,512]{1,0:T(2,128)(2,1)}, u32[]{:S(2)}) copy-start(bf16[1,512]{1,0:T(2,128)(2,1)} %assay.1) | copy-start | bytes 3076
  166.6 1.3 copy-start.1

commit v6 on v3

--- a/solution.py
+++ b/solution.py
@@ -1,3 +1,4 @@
+import functools
 import math
 
 import jax
@@ -236,12 +237,15 @@
             recv_sem=recvs.at[s, slot], device_id={"narrow": peer}, device_id_type=MESH,
         )
 
-    def send_all(make, count, me, args, s):
+    def code_and_send(code, make, count, me, args, s):
         def one(i, _):
-            make(*args, s, lax.rem(me + i, count), me).start()
+            peer = lax.rem(me + i, count)
+            code(peer)
+            make(*args, s, peer, me).start()
             return 0
 
         lax.fori_loop(1, count, one, 0)
+        code(me)
 
     def recv_all(make, count, me, args, s):
         def one(i, _):
@@ -439,13 +443,11 @@
             at = rows((s * 32 + w) * 32, 32)
             return zre[at, :], zim[at, :]
 
-        def code_one(w, _, s=s, read=read_depth):
+        def code_one(w, s=s, read=read_depth):
             code_wide(read, ws, s, w, w)
-            return 0
-
-        lax.fori_loop(0, WIDE, code_one, 0)
+
+        code_and_send(code_one, wide_copy, WIDE, me_w, w_args, s)
         wr[s, me_w] = ws[s, me_w]
-        send_all(wide_copy, WIDE, me_w, w_args, s)
 
     def second_forward(s, p, q, r):
         def group(g, _):
@@ -512,38 +514,34 @@
         else:
             second_forward(s, None, None, None)
 
-        def code_n(n, _, s=s):
-            code_narrow(s, n)
-            return 0
-
-        lax.fori_loop(0, NARROW, code_n, 0)
+        code_and_send(functools.partial(code_narrow, s), narrow_copy, NARROW, me_n, n_args, s)
         nr[s, me_n] = ns[s, me_n]
-        send_all(narrow_copy, NARROW, me_n, n_args, s)
-
-
-    lax.fori_loop(1, NARROW, recv_measures, 0)
-    row = lax.broadcasted_iota(i32, (512, room), 0)
-    want = (((row >> 4) << 3) + (row & 7) + 1).astype(f32)
-    flags = precv[0].astype(f32)
-    for k in range(1, NARROW):
-        flags = jnp.maximum(flags, precv[k].astype(f32))
-    flags = jnp.max(jnp.where(flag_row, flags, 0.0), axis=1, keepdims=True)
-    flags = jnp.max(flags, axis=0, keepdims=True)
-    flag_col = lax.broadcasted_iota(i32, (512, 128), 1) == 13
-    for q in range(4):
-        moved, named = 0.0, 0.0
-        for k in range(2):
-            key = precv[2 * q + k, 0:1, :].astype(f32)
-            match = (((row >> 3) & 1) == k) & (want == key)
-            hot = jnp.where(match, 1.0, 0.0).astype(bf16)
-            moved = moved + mm(hot, arecv[2 * q + k])
-            named = named + mm_t(hot, precv[2 * q + k])
-        named = jnp.concatenate([named, jnp.zeros((512, 112), f32)], axis=1)
-        named = jnp.where(flag_col, flags, named)
-        bsend[:, 16 * q : 16 * q + 16, 0:512] = moved.astype(bf16).reshape(WIDE, 16, 512)
-        bsend[:, 16 * q : 16 * q + 16, 512:640] = named.astype(bf16).reshape(WIDE, 16, 128)
-    brecv[me_w] = bsend[me_w]
-    lax.fori_loop(1, WIDE, send_groups, 0)
+
+
+    def regroup():
+        lax.fori_loop(1, NARROW, recv_measures, 0)
+        row = lax.broadcasted_iota(i32, (512, room), 0)
+        want = (((row >> 4) << 3) + (row & 7) + 1).astype(f32)
+        flags = precv[0].astype(f32)
+        for k in range(1, NARROW):
+            flags = jnp.maximum(flags, precv[k].astype(f32))
+        flags = jnp.max(jnp.where(flag_row, flags, 0.0), axis=1, keepdims=True)
+        flags = jnp.max(flags, axis=0, keepdims=True)
+        flag_col = lax.broadcasted_iota(i32, (512, 128), 1) == 13
+        for q in range(4):
+            moved, named = 0.0, 0.0
+            for k in range(2):
+                key = precv[2 * q + k, 0:1, :].astype(f32)
+                match = (((row >> 3) & 1) == k) & (want == key)
+                hot = jnp.where(match, 1.0, 0.0).astype(bf16)
+                moved = moved + mm(hot, arecv[2 * q + k])
+                named = named + mm_t(hot, precv[2 * q + k])
+            named = jnp.concatenate([named, jnp.zeros((512, 112), f32)], axis=1)
+            named = jnp.where(flag_col, flags, named)
+            bsend[:, 16 * q : 16 * q + 16, 0:512] = moved.astype(bf16).reshape(WIDE, 16, 512)
+            bsend[:, 16 * q : 16 * q + 16, 512:640] = named.astype(bf16).reshape(WIDE, 16, 128)
+        brecv[me_w] = bsend[me_w]
+        lax.fori_loop(1, WIDE, send_groups, 0)
 
     total = 1.0 / (NX * NY * NZ)
     v_main.wait_recv()
@@ -653,24 +651,26 @@
             return 0
 
         lax.fori_loop(0, 8, unblock, 0)
-        for n in range(8):
-            base = 128 * (n % 2)
-            tiles = [
-                (big2[n // 2, base + 8 * k : base + 8 * k + 8, 0:128],
-                 big2[n // 2, base + 8 * k : base + 8 * k + 8, 128:256])
-                for k in range(16)
-            ]
-            code = scale_code(tile_max([x for pair in tiles for x in pair]))
-            fac = encode_factor(code)
-            for k, (re, im) in enumerate(tiles):
-                ms[s, n, 8 * k : 8 * k + 8, :] = pack(re * fac, im * fac)
-            ms[s, n, 128:136, :] = code
+
+    def code_first(s, n):
+        page, base = lax.div(n, 2), 128 * lax.rem(n, 2)
+        tiles = []
+        for k in range(16):
+            at = rows(base + 8 * k, 8)
+            tiles.append((big2[page, at, 0:128], big2[page, at, 128:256]))
+        code = scale_code(tile_max([x for pair in tiles for x in pair]))
+        fac = encode_factor(code)
+        for k, (re, im) in enumerate(tiles):
+            ms[s, n, 8 * k : 8 * k + 8, :] = pack(re * fac, im * fac)
+        ms[s, n, 128:136, :] = code
 
     for s in range(SLOTS):
         recv_all(narrow_copy, NARROW, me_n, n_args, s)
         first_both(s)
+        code_and_send(functools.partial(code_first, s), narrow_copy, NARROW, me_n, m_args, s)
         mr[s, me_n] = ms[s, me_n]
-        send_all(narrow_copy, NARROW, me_n, m_args, s)
+        if s == 0:
+            regroup()
 
     row16 = lax.broadcasted_iota(i32, (16, 128), 0)
 
@@ -740,14 +740,12 @@
             at = rows((b % 2) * 128 + (w % 4) * 32, 32)
             return big2[b // 2, at, 0:128], big2[b // 2, at, 128:256]
 
-        def code_back(w, _, s=s):
+        def code_back(w, s=s):
             code_wide(read_back, us, s, w, w)
-            return 0
-
-        lax.fori_loop(0, WIDE, code_back, 0)
+
+        code_and_send(code_back, wide_copy, WIDE, me_w, u_args, s)
         keep = pltpu.make_async_copy(us.at[s, me_w], out.at[s, me_w], u_recv.at[s, me_w])
         keep.start()
-        send_all(wide_copy, WIDE, me_w, u_args, s)
 
     lax.fori_loop(1, WIDE, recv_groups, 0)
     pltpu.make_async_copy(brecv, got, g_sem.at[0]).start()
@@ -758,7 +756,7 @@
         listed = jnp.round(mm_t(join[...], named))
         numbers[g] = listed.astype(i32)
         marks = listed if g == 0 else jnp.maximum(marks, listed)
-    flag[...] = jnp.broadcast_to(jnp.max(marks, axis=1, keepdims=True), (8, 128)).astype(i32)
+    flag[0, 0] = jnp.max(marks[5:6, :]).astype(i32)
     lax.fori_loop(1, WIDE, sent_groups, 0)
     lax.fori_loop(1, NARROW, sent_measures, 0)
     pltpu.make_async_copy(brecv, got, g_sem.at[0]).wait()
@@ -790,10 +788,13 @@
             jax.ShapeDtypeStruct((SLOTS, WIDE, 40, 128), i32),
             jax.ShapeDtypeStruct((WIDE, 64, 640), bf16),
             jax.ShapeDtypeStruct((16, 8, 128), i32),
-            jax.ShapeDtypeStruct((8, 128), i32),
+            jax.ShapeDtypeStruct((1, 1), i32),
         ),
         in_specs=[vmem] * 19,
-        out_specs=(pl.BlockSpec(memory_space=pl.ANY), pl.BlockSpec(memory_space=pl.ANY), vmem, vmem),
+        out_specs=(
+            pl.BlockSpec(memory_space=pl.ANY), pl.BlockSpec(memory_space=pl.ANY), vmem,
+            pl.BlockSpec(memory_space=pltpu.SMEM),
+        ),
         scratch_shapes=[
             pltpu.VMEM((2048, 128), f32),
             pltpu.VMEM((2048, 128), f32),
@@ -954,7 +955,7 @@
         more = padded(assay[0], weights, measure_owner[0], measure_cell[0], measure_pencils[0])
         return finish(freq, *more)
 
-    field = lax.cond(flag[5, 0] > 0, roomy, lambda _: finish(freq, held, numbers), 0)
+    field = lax.cond(flag[0, 0] > 0, roomy, lambda _: finish(freq, held, numbers), 0)
     return field.reshape(noise.shape)
 
 

time: 161 us -> 176 us (1.093)
  Pallas kernels: 157 us -> 173 us
    pallas_call x1, Pallas kernels: 135 us -> 152 us  [spectral(): pl.pallas_call(spectral_kernel, out_shape=(jax.ShapeDtypeStruct((SLOTS, W...]
where the time goes in v6:
time: 176 us
  Pallas kernels  173 us (98%)
    pallas_call x1, Pallas kernels, spectral(): pl.pallas_call(spectral_kernel, out_shape=(jax.ShapeDtypeStruct((SLOTS, W...  152 us
    pallas_call x1, Pallas kernels, finish(): pl.pallas_call(finish_kernel, out_shape=jax.ShapeDtypeStruct((4096, 128),...  21.6 us

profile of v6, /device:TPU:65, one launch (start us, length us, event | category | flops | bytes accessed | tf_op | source)
XLA Modules:
  0.0 175.5 jit_solution(8346808892674350859)
XLA Ops:
  0.0 0.0 copy-start.2
  0.0 0.0 copy-start.3
  0.0 0.0 copy-start.4
  0.0 0.0 copy-start.5
  0.0 0.0 copy-start.6
  0.0 151.8 %shard_map.202 = (s32[2,32,40,128]{3,2,1,0:T(8,128)S(1)}, bf16[32,64,640]{2,1,0:T(8,128)(2,1)S(1)}, s32[16,8,128]{2,1,0:T(8,128)S(1)}, s32[1,1]{1,0:T(1,128)}) custom-call(f32[4096,128]{1,0:T(8,128)} %bitcast.52, f32[4096,128]{1,0:T(8,128)} %bitcast.53, bf16[128,384]{1,0:T(8,128)(2,1)} %constant.156.clone.tz, bf16[2,256,256]{2,1,0:T(8,128)(2,1)} %constant.157.clone.yf.xi, ...), custom_call_target="tpu_custom_call" | custom-call | tf_op jit(solution)/shard_map/pallas_call | solution.py:785
  152.5 0.0 copy-done.2
  152.5 0.0 copy-done.3
  152.5 0.0 copy-done.4
  152.5 0.0 copy-done.5
  152.5 0.0 copy-done.6
  152.5 21.7 %conditional.1 = (f32[128,32,128]{2,1,0:T(8,128)S(1)}) conditional(s32[]{:T(128)} %bitcast.21, (s32[2,32,40,128]{3,2,1,0:T(8,128)S(1)}, bf16[32,64,640]{2,1,0:T(8,128)(2,1)S(1)}, s32[16,8,128]{2,1,0:T(8,128)S(1)}, bf16[384,128]{1,0:T(8,128)(2,1)S(1)}) %tuple.45, (s32[1,512]{1,0:T(1,128)S(1)}, bf16[1,512,4,128]{3,2,1,0:T(4,128)(2,1)}, ...), branch_computations={%region_0.0_spmd, %region_1.4_spmd} | conditional | flops 1373095424 | bytes 37477444 | solution.py:958
  152.6 21.6 %branch_0_fun.1 = f32[4096,128]{1,0:T(8,128)S(1)} custom-call(s32[16,8,128]{2,1,0:T(8,128)S(1)} %get-tuple-element.45.numbers, s32[2560,128]{1,0:T(8,128)S(1)} %bitcast.45, bf16[384,128]{1,0:T(8,128)(2,1)S(1)} %get-tuple-element.47.tzi, bf16[2048,640]{1,0:T(8,128)(2,1)S(1)} %bitcast.47), custom_call_target="tpu_custom_call" | custom-call | tf_op jit(solution)/shard_map/cond/branch_0_fun/pallas_call | solution.py:910
  174.2 0.0 copy-start.1
  174.2 1.3 copy-done.1
Async XLA Ops:
  0.0 152.5 %copy-start.2 = (bf16[384,128]{1,0:T(8,128)(2,1)S(1)}, bf16[384,128]{1,0:T(8,128)(2,1)}, u32[]{:S(2)}) copy-start(bf16[384,128]{1,0:T(8,128)(2,1)} %constant.167.clone) | copy-start | bytes 294916
  0.0 152.5 %copy-start.3 = (s32[1,512,4]{1,2,0:T(4,128)S(1)}, s32[1,512,4]{1,2,0:T(4,128)}, u32[]{:S(2)}) copy-start(s32[1,512,4]{1,2,0:T(4,128)} %param.31) | copy-start | bytes 24580
  0.0 152.5 %copy-start.4 = (s32[1,512]{1,0:T(1,128)S(1)}, s32[1,512]{1,0:T(1,128)}, u32[]{:S(2)}) copy-start(s32[1,512]{1,0:T(1,128)} %owner.1) | copy-start | bytes 6148
  0.0 152.5 %copy-start.5 = (s32[1,512]{1,0:T(1,128)S(1)}, s32[1,512]{1,0:T(1,128)}, u32[]{:S(2)}) copy-start(s32[1,512]{1,0:T(1,128)} %cell.1) | copy-start | bytes 6148
  0.0 152.5 %copy-start.6 = (bf16[1,512]{1,0:T(2,128)(2,1)S(1)}, bf16[1,512]{1,0:T(2,128)(2,1)}, u32[]{:S(2)}) copy-start(bf16[1,512]{1,0:T(2,128)(2,1)} %assay.1) | copy-start | bytes 3076
  174.2 1.3 copy-start.1

commit v7 on v6

--- a/solution.py
+++ b/solution.py
@@ -543,6 +543,8 @@
         brecv[me_w] = bsend[me_w]
         lax.fori_loop(1, WIDE, send_groups, 0)
 
+    regroup()
+
     total = 1.0 / (NX * NY * NZ)
     v_main.wait_recv()
 
@@ -669,8 +671,6 @@
         first_both(s)
         code_and_send(functools.partial(code_first, s), narrow_copy, NARROW, me_n, m_args, s)
         mr[s, me_n] = ms[s, me_n]
-        if s == 0:
-            regroup()
 
     row16 = lax.broadcasted_iota(i32, (16, 128), 0)
 

time: 176 us -> 159 us (0.903)
  Pallas kernels: 173 us -> 156 us
    pallas_call x1, Pallas kernels: 152 us -> 134 us  [spectral(): pl.pallas_call(spectral_kernel, out_shape=(jax.ShapeDtypeStruct((SLOTS, W...]
where the time goes in v7:
time: 159 us; the launch traced here: 158 us
  Pallas kernels  156 us (98%)
    pallas_call x1, Pallas kernels, spectral(): pl.pallas_call(spectral_kernel, out_shape=(jax.ShapeDtypeStruct((SLOTS, W...  134 us
    pallas_call x1, Pallas kernels, finish(): pl.pallas_call(finish_kernel, out_shape=jax.ShapeDtypeStruct((4096, 128),...  21.8 us

profile of v7, /device:TPU:65, one launch (start us, length us, event | category | flops | bytes accessed | tf_op | source)
XLA Modules:
  0.0 157.9 jit_solution(14228060168546153102)
XLA Ops:
  0.0 0.0 copy-start.2
  0.0 0.0 copy-start.3
  0.0 0.0 copy-start.4
  0.0 0.0 copy-start.5
  0.0 0.0 copy-start.6
  0.0 134.1 %shard_map.202 = (s32[2,32,40,128]{3,2,1,0:T(8,128)S(1)}, bf16[32,64,640]{2,1,0:T(8,128)(2,1)S(1)}, s32[16,8,128]{2,1,0:T(8,128)S(1)}, s32[1,1]{1,0:T(1,128)}) custom-call(f32[4096,128]{1,0:T(8,128)} %bitcast.52, f32[4096,128]{1,0:T(8,128)} %bitcast.53, bf16[128,384]{1,0:T(8,128)(2,1)} %constant.156.clone.tz, bf16[2,256,256]{2,1,0:T(8,128)(2,1)} %constant.157.clone.yf.xi, ...), custom_call_target="tpu_custom_call" | custom-call | tf_op jit(solution)/shard_map/pallas_call | solution.py:785
  134.7 0.0 copy-done.2
  134.7 0.0 copy-done.3
  134.8 0.0 copy-done.4
  134.8 0.0 copy-done.5
  134.8 0.0 copy-done.6
  134.8 21.8 %conditional.1 = (f32[128,32,128]{2,1,0:T(8,128)S(1)}) conditional(s32[]{:T(128)} %bitcast.21, (s32[2,32,40,128]{3,2,1,0:T(8,128)S(1)}, bf16[32,64,640]{2,1,0:T(8,128)(2,1)S(1)}, s32[16,8,128]{2,1,0:T(8,128)S(1)}, bf16[384,128]{1,0:T(8,128)(2,1)S(1)}) %tuple.45, (s32[1,512]{1,0:T(1,128)S(1)}, bf16[1,512,4,128]{3,2,1,0:T(4,128)(2,1)}, ...), branch_computations={%region_0.0_spmd, %region_1.4_spmd} | conditional | flops 1373095424 | bytes 37477444 | solution.py:958
  134.8 21.8 %branch_0_fun.1 = f32[4096,128]{1,0:T(8,128)S(1)} custom-call(s32[16,8,128]{2,1,0:T(8,128)S(1)} %get-tuple-element.45.numbers, s32[2560,128]{1,0:T(8,128)S(1)} %bitcast.45, bf16[384,128]{1,0:T(8,128)(2,1)S(1)} %get-tuple-element.47.tzi, bf16[2048,640]{1,0:T(8,128)(2,1)S(1)} %bitcast.47), custom_call_target="tpu_custom_call" | custom-call | tf_op jit(solution)/shard_map/cond/branch_0_fun/pallas_call | solution.py:910
  156.6 0.0 copy-start.1
  156.6 1.3 copy-done.1
Async XLA Ops:
  0.0 134.7 %copy-start.2 = (bf16[384,128]{1,0:T(8,128)(2,1)S(1)}, bf16[384,128]{1,0:T(8,128)(2,1)}, u32[]{:S(2)}) copy-start(bf16[384,128]{1,0:T(8,128)(2,1)} %constant.167.clone) | copy-start | bytes 294916
  0.0 134.7 %copy-start.3 = (s32[1,512,4]{1,2,0:T(4,128)S(1)}, s32[1,512,4]{1,2,0:T(4,128)}, u32[]{:S(2)}) copy-start(s32[1,512,4]{1,2,0:T(4,128)} %param.31) | copy-start | bytes 24580
  0.0 134.8 %copy-start.4 = (s32[1,512]{1,0:T(1,128)S(1)}, s32[1,512]{1,0:T(1,128)}, u32[]{:S(2)}) copy-start(s32[1,512]{1,0:T(1,128)} %owner.1) | copy-start | bytes 6148
  0.0 134.8 %copy-start.5 = (s32[1,512]{1,0:T(1,128)S(1)}, s32[1,512]{1,0:T(1,128)}, u32[]{:S(2)}) copy-start(s32[1,512]{1,0:T(1,128)} %cell.1) | copy-start | bytes 6148
  0.0 134.8 %copy-start.6 = (bf16[1,512]{1,0:T(2,128)(2,1)S(1)}, bf16[1,512]{1,0:T(2,128)(2,1)}, u32[]{:S(2)}) copy-start(bf16[1,512]{1,0:T(2,128)(2,1)} %assay.1) | copy-start | bytes 3076
  156.6 1.3 copy-start.1

commit v8 on v7

--- a/solution.py
+++ b/solution.py
@@ -268,43 +268,6 @@
     m_args = (ms, mr, m_send, m_recv)
     u_args = (us, out, u_send, u_recv)
 
-    late = special & (me_n >= 4)
-    own_slots = (jnp.where(late, 2, 0), 1)
-    mir_slots = (jnp.where(special & (me_n < 4), 2, jnp.where(special, 0, 2)), 3)
-
-    def spectrum_rows(slot, e):
-        return halves(spec[pl.ds(slot * 1024 + e, 128, stride=8), :])
-
-    for e in range(8):
-        back = (8 - e) % 8
-        flip = flips[0 if e == 0 else 1]
-        codes = []
-        for s in range(SLOTS):
-            h, l = spectrum_rows(own_slots[s], e)
-            ear[s, e] = mm_t(own2[...], jnp.concatenate([h, l], axis=1))
-            h, l = spectrum_rows(mir_slots[s], back)
-            gh = mm_t(mir[...], h).astype(bf16)
-            gl = mm_t(mir[...], l).astype(bf16)
-            v = mm(jnp.concatenate([gh, gl], axis=1), flip)
-            q = jnp.round((jnp.log(v) - SPEC_LOW) * SPEC_CODE - 32500.0)
-            codes.append(jnp.clip(q, -32767.0, 32767.0))
-        vs[e] = pack(codes[0], codes[1])
-
-    v_main = pltpu.make_async_remote_copy(
-        src_ref=vs, dst_ref=vr, send_sem=v_send.at[0], recv_sem=v_recv.at[0],
-        device_id={"narrow": 7 - me_n}, device_id_type=MESH,
-    )
-    v_side = pltpu.make_async_remote_copy(
-        src_ref=vs.at[:, pl.ds(0, 8), :], dst_ref=vc, send_sem=v_send.at[1], recv_sem=v_recv.at[1],
-        device_id={"narrow": lax.rem(8 - me_n, 8)}, device_id_type=MESH,
-    )
-
-    alone = (me_n == 0) | (me_n == 4)
-
-    @pl.when(alone)
-    def _():
-        vc[...] = vs[:, 0:8, :]
-
     room = asend.shape[1]
     count = owner.shape[1]
     owners = owner[...]
@@ -408,6 +371,44 @@
 
     pl.semaphore_wait(barrier, WIDE - 1 + NARROW - 1)
     lax.fori_loop(1, NARROW, send_measures, 0)
+
+    late = special & (me_n >= 4)
+    own_slots = (jnp.where(late, 2, 0), 1)
+    mir_slots = (jnp.where(special & (me_n < 4), 2, jnp.where(special, 0, 2)), 3)
+
+    def spectrum_rows(slot, e):
+        return halves(spec[pl.ds(slot * 1024 + e, 128, stride=8), :])
+
+    for e in range(8):
+        back = (8 - e) % 8
+        flip = flips[0 if e == 0 else 1]
+        codes = []
+        for s in range(SLOTS):
+            h, l = spectrum_rows(own_slots[s], e)
+            ear[s, e] = mm_t(own2[...], jnp.concatenate([h, l], axis=1))
+            h, l = spectrum_rows(mir_slots[s], back)
+            gh = mm_t(mir[...], h).astype(bf16)
+            gl = mm_t(mir[...], l).astype(bf16)
+            v = mm(jnp.concatenate([gh, gl], axis=1), flip)
+            q = jnp.round((jnp.log(v) - SPEC_LOW) * SPEC_CODE - 32500.0)
+            codes.append(jnp.clip(q, -32767.0, 32767.0))
+        vs[e] = pack(codes[0], codes[1])
+
+    v_main = pltpu.make_async_remote_copy(
+        src_ref=vs, dst_ref=vr, send_sem=v_send.at[0], recv_sem=v_recv.at[0],
+        device_id={"narrow": 7 - me_n}, device_id_type=MESH,
+    )
+    v_side = pltpu.make_async_remote_copy(
+        src_ref=vs.at[:, pl.ds(0, 8), :], dst_ref=vc, send_sem=v_send.at[1], recv_sem=v_recv.at[1],
+        device_id={"narrow": lax.rem(8 - me_n, 8)}, device_id_type=MESH,
+    )
+
+    alone = (me_n == 0) | (me_n == 4)
+
+    @pl.when(alone)
+    def _():
+        vc[...] = vs[:, 0:8, :]
+
     v_main.start()
 
     @pl.when(jnp.logical_not(alone))
@@ -848,15 +849,19 @@
         acc[...] = jnp.zeros_like(acc)
 
     def depth(g, _):
+        pieces = []
         for j in range(4):
             y = g * 4 + j
             re, im = unpack(freq[pl.ds(y, 64, stride=40), :])
             d = decode_factor(freq[pl.ds(32 + lax.rem(y, 8), 64, stride=40), :])
             h, l = halves(jnp.concatenate([re * d, im * d], axis=0))
-            u = jnp.concatenate([h, h, l], axis=0)
-            out[pl.ds(y, 128, stride=32), :] = lax.dot_general(
-                u, tzi[...], (((0,), (0,)), ((), ())), preferred_element_type=f32
-            )
+            pieces.append(jnp.concatenate([h, h, l], axis=0))
+        cells = lax.dot_general(
+            jnp.concatenate(pieces, axis=1), tzi[...], (((0,), (0,)), ((), ())),
+            preferred_element_type=f32,
+        )
+        for j in range(4):
+            out[pl.ds(g * 4 + j, 128, stride=32), :] = cells[128 * j : 128 * j + 128]
         return 0
 
     lax.fori_loop(0, 8, depth, 0)

time: 159 us -> 157 us (0.987)
  Pallas kernels: 156 us -> 153 us
    pallas_call x1, Pallas kernels: 134 us -> 131 us  [spectral(): pl.pallas_call(spectral_kernel, out_shape=(jax.ShapeDtypeStruct((SLOTS, W...]
where the time goes in v8:
time: 157 us; the launch traced here: 155 us
  Pallas kernels  153 us (97%)
    pallas_call x1, Pallas kernels, spectral(): pl.pallas_call(spectral_kernel, out_shape=(jax.ShapeDtypeStruct((SLOTS, W...  131 us
    pallas_call x1, Pallas kernels, finish(): pl.pallas_call(finish_kernel, out_shape=jax.ShapeDtypeStruct((4096, 128),...  21.8 us

profile of v8, /device:TPU:65, one launch (start us, length us, event | category | flops | bytes accessed | tf_op | source)
XLA Modules:
  0.0 154.8 jit_solution(8782300855092657370)
XLA Ops:
  0.0 0.0 copy-start.2
  0.0 0.0 copy-start.3
  0.0 0.0 copy-start.4
  0.0 0.0 copy-start.5
  0.0 0.0 copy-start.6
  0.0 130.9 %shard_map.202 = (s32[2,32,40,128]{3,2,1,0:T(8,128)S(1)}, bf16[32,64,640]{2,1,0:T(8,128)(2,1)S(1)}, s32[16,8,128]{2,1,0:T(8,128)S(1)}, s32[1,1]{1,0:T(1,128)}) custom-call(f32[4096,128]{1,0:T(8,128)} %bitcast.52, f32[4096,128]{1,0:T(8,128)} %bitcast.53, bf16[128,384]{1,0:T(8,128)(2,1)} %constant.156.clone.tz, bf16[2,256,256]{2,1,0:T(8,128)(2,1)} %constant.157.clone.yf.xi, ...), custom_call_target="tpu_custom_call" | custom-call | tf_op jit(solution)/shard_map/pallas_call | solution.py:786
  131.6 0.0 copy-done.2
  131.6 0.0 copy-done.3
  131.6 0.0 copy-done.4
  131.6 0.0 copy-done.5
  131.6 0.0 copy-done.6
  131.6 21.8 %conditional.1 = (f32[128,32,128]{2,1,0:T(8,128)S(1)}) conditional(s32[]{:T(128)} %bitcast.21, (s32[2,32,40,128]{3,2,1,0:T(8,128)S(1)}, bf16[32,64,640]{2,1,0:T(8,128)(2,1)S(1)}, s32[16,8,128]{2,1,0:T(8,128)S(1)}, bf16[384,128]{1,0:T(8,128)(2,1)S(1)}) %tuple.45, (s32[1,512]{1,0:T(1,128)S(1)}, bf16[1,512,4,128]{3,2,1,0:T(4,128)(2,1)}, ...), branch_computations={%region_0.0_spmd, %region_1.4_spmd} | conditional | flops 1373095424 | bytes 37477444 | solution.py:963
  131.7 21.8 %branch_0_fun.1 = f32[4096,128]{1,0:T(8,128)S(1)} custom-call(s32[16,8,128]{2,1,0:T(8,128)S(1)} %get-tuple-element.45.numbers, s32[2560,128]{1,0:T(8,128)S(1)} %bitcast.45, bf16[384,128]{1,0:T(8,128)(2,1)S(1)} %get-tuple-element.47.tzi, bf16[2048,640]{1,0:T(8,128)(2,1)S(1)} %bitcast.47), custom_call_target="tpu_custom_call" | custom-call | tf_op jit(solution)/shard_map/cond/branch_0_fun/pallas_call | solution.py:915
  153.5 0.0 copy-start.1
  153.5 1.3 copy-done.1
Async XLA Ops:
  0.0 131.6 %copy-start.2 = (bf16[384,128]{1,0:T(8,128)(2,1)S(1)}, bf16[384,128]{1,0:T(8,128)(2,1)}, u32[]{:S(2)}) copy-start(bf16[384,128]{1,0:T(8,128)(2,1)} %constant.167.clone) | copy-start | bytes 294916
  0.0 131.6 %copy-start.3 = (s32[1,512,4]{1,2,0:T(4,128)S(1)}, s32[1,512,4]{1,2,0:T(4,128)}, u32[]{:S(2)}) copy-start(s32[1,512,4]{1,2,0:T(4,128)} %param.31) | copy-start | bytes 24580
  0.0 131.6 %copy-start.4 = (s32[1,512]{1,0:T(1,128)S(1)}, s32[1,512]{1,0:T(1,128)}, u32[]{:S(2)}) copy-start(s32[1,512]{1,0:T(1,128)} %owner.1) | copy-start | bytes 6148
  0.0 131.6 %copy-start.5 = (s32[1,512]{1,0:T(1,128)S(1)}, s32[1,512]{1,0:T(1,128)}, u32[]{:S(2)}) copy-start(s32[1,512]{1,0:T(1,128)} %cell.1) | copy-start | bytes 6148
  0.0 131.6 %copy-start.6 = (bf16[1,512]{1,0:T(2,128)(2,1)S(1)}, bf16[1,512]{1,0:T(2,128)(2,1)}, u32[]{:S(2)}) copy-start(bf16[1,512]{1,0:T(2,128)(2,1)} %assay.1) | copy-start | bytes 3076
  153.5 1.3 copy-start.1

commit v9 on v8

--- a/solution.py
+++ b/solution.py
@@ -845,10 +845,9 @@
 
 
 def finish_kernel(numbers, freq, tzi, held, out, gathered, contrib, *accs):
-    for acc in accs:
-        acc[...] = jnp.zeros_like(acc)
-
     def depth(g, _):
+        for acc in accs:
+            acc[rows(g * 512, 512), :] = jnp.zeros((512, 128), f32)
         pieces = []
         for j in range(4):
             y = g * 4 + j

time: 157 us -> 157 us (level)
  no operation moved by 1% of the time
where the time goes in v9:
time: 157 us; the launch traced here: 155 us
  Pallas kernels  153 us (97%)
    pallas_call x1, Pallas kernels, spectral(): pl.pallas_call(spectral_kernel, out_shape=(jax.ShapeDtypeStruct((SLOTS, W...  131 us
    pallas_call x1, Pallas kernels, finish(): pl.pallas_call(finish_kernel, out_shape=jax.ShapeDtypeStruct((4096, 128),...  21.7 us

profile of v9, /device:TPU:65, one launch (start us, length us, event | category | flops | bytes accessed | tf_op | source)
XLA Modules:
  0.0 154.7 jit_solution(180579979056687830)
XLA Ops:
  0.0 0.0 copy-start.2
  0.0 0.0 copy-start.3
  0.0 0.0 copy-start.4
  0.0 0.0 copy-start.5
  0.0 0.0 copy-start.6
  0.0 130.9 %shard_map.202 = (s32[2,32,40,128]{3,2,1,0:T(8,128)S(1)}, bf16[32,64,640]{2,1,0:T(8,128)(2,1)S(1)}, s32[16,8,128]{2,1,0:T(8,128)S(1)}, s32[1,1]{1,0:T(1,128)}) custom-call(f32[4096,128]{1,0:T(8,128)} %bitcast.52, f32[4096,128]{1,0:T(8,128)} %bitcast.53, bf16[128,384]{1,0:T(8,128)(2,1)} %constant.156.clone.tz, bf16[2,256,256]{2,1,0:T(8,128)(2,1)} %constant.157.clone.yf.xi, ...), custom_call_target="tpu_custom_call" | custom-call | tf_op jit(solution)/shard_map/pallas_call | solution.py:786
  131.6 0.0 copy-done.2
  131.6 0.0 copy-done.3
  131.6 0.0 copy-done.4
  131.6 0.0 copy-done.5
  131.6 0.0 copy-done.6
  131.6 21.7 %conditional.1 = (f32[128,32,128]{2,1,0:T(8,128)S(1)}) conditional(s32[]{:T(128)} %bitcast.21, (s32[2,32,40,128]{3,2,1,0:T(8,128)S(1)}, bf16[32,64,640]{2,1,0:T(8,128)(2,1)S(1)}, s32[16,8,128]{2,1,0:T(8,128)S(1)}, bf16[384,128]{1,0:T(8,128)(2,1)S(1)}) %tuple.45, (s32[1,512]{1,0:T(1,128)S(1)}, bf16[1,512,4,128]{3,2,1,0:T(4,128)(2,1)}, ...), branch_computations={%region_0.0_spmd, %region_1.4_spmd} | conditional | flops 1373095424 | bytes 37477444 | solution.py:962
  131.7 21.7 %branch_0_fun.1 = f32[4096,128]{1,0:T(8,128)S(1)} custom-call(s32[16,8,128]{2,1,0:T(8,128)S(1)} %get-tuple-element.45.numbers, s32[2560,128]{1,0:T(8,128)S(1)} %bitcast.45, bf16[384,128]{1,0:T(8,128)(2,1)S(1)} %get-tuple-element.47.tzi, bf16[2048,640]{1,0:T(8,128)(2,1)S(1)} %bitcast.47), custom_call_target="tpu_custom_call" | custom-call | tf_op jit(solution)/shard_map/cond/branch_0_fun/pallas_call | solution.py:914
  153.4 0.0 copy-start.1
  153.4 1.3 copy-done.1
Async XLA Ops:
  0.0 131.6 %copy-start.2 = (bf16[384,128]{1,0:T(8,128)(2,1)S(1)}, bf16[384,128]{1,0:T(8,128)(2,1)}, u32[]{:S(2)}) copy-start(bf16[384,128]{1,0:T(8,128)(2,1)} %constant.167.clone) | copy-start | bytes 294916
  0.0 131.6 %copy-start.3 = (s32[1,512,4]{1,2,0:T(4,128)S(1)}, s32[1,512,4]{1,2,0:T(4,128)}, u32[]{:S(2)}) copy-start(s32[1,512,4]{1,2,0:T(4,128)} %param.31) | copy-start | bytes 24580
  0.0 131.6 %copy-start.4 = (s32[1,512]{1,0:T(1,128)S(1)}, s32[1,512]{1,0:T(1,128)}, u32[]{:S(2)}) copy-start(s32[1,512]{1,0:T(1,128)} %owner.1) | copy-start | bytes 6148
  0.0 131.6 %copy-start.5 = (s32[1,512]{1,0:T(1,128)S(1)}, s32[1,512]{1,0:T(1,128)}, u32[]{:S(2)}) copy-start(s32[1,512]{1,0:T(1,128)} %cell.1) | copy-start | bytes 6148
  0.0 131.6 %copy-start.6 = (bf16[1,512]{1,0:T(2,128)(2,1)S(1)}, bf16[1,512]{1,0:T(2,128)(2,1)}, u32[]{:S(2)}) copy-start(bf16[1,512]{1,0:T(2,128)(2,1)} %assay.1) | copy-start | bytes 3076
  153.4 1.3 copy-start.1
